TPU v7x, 128 devices: a whole 4x4x4 slice. The times are simulated.
128 devices in a mesh: ctx: 32 (over y, x, core), head: 4 (over z), rep: 1.
Axes of the slice: x: 4, y: 4, z: 4, core: 2. Of those that a mesh axis runs over, the one named last changes fastest.
Arguments:
- queries: bfloat16 [32768, 4096], P(('rep', 'ctx'), 'head'), may hold values from -6 to 6
- keys: bfloat16 [32768, 512], P(('rep', 'ctx'), 'head'), may hold values from -6 to 6
- values: bfloat16 [32768, 512], P(('rep', 'ctx'), 'head'), may hold values from -6 to 6
- grad_out: bfloat16 [32768, 4096], P(('rep', 'ctx'), 'head'), may hold values from -48 to 48
- ancestor_ids: int32 [256, 6], P(('rep', 'ctx')), may hold values from 0 to 255, as said below
- ancestor_count: int32 [256], P(('rep', 'ctx')), may hold values from 0 to 6, as said below
Outputs:
- grad_queries: bfloat16 [32768, 4096], P(('rep', 'ctx'), 'head')
- grad_keys: bfloat16 [32768, 512], P(('rep', 'ctx'), 'head')
- grad_values: bfloat16 [32768, 512], P(('rep', 'ctx'), 'head')
Inputs may be any that keep to these rules, and one draw needn't show every extreme that they name: The blocks are the nodes of a tree in depth-first order: block 0 is the root, and the parent of every other block b is block b - 1 or one of its ancestors. For j below ancestor_count[b], ancestor_ids[b, j] is the ancestor of block b at depth j (the root first, then ever deeper); entries past the count are 0. ancestor_count[b] is the depth of block b; some block has 6 ancestors.
All inputs are finite; a program needn't handle non-finite values.
Results may differ from a plain program's by a relative error of at most 0.0052.
Values may be sent and summed in bfloat16 or wider, within the bound.
No kernel may reach another device: no remote copies, remote signals or barrier semaphores. Data moves between devices by JAX's collectives and lax.ppermute only.
A program may use at most 256 MiB of HBM per device.

v0:
```python
import jax
import jax.numpy as jnp
from jax import lax
from jax.sharding import PartitionSpec as P

HD = 128
HQ_KV = 8
BLK = 128
MAXA = 6


def tile_mask(is_live):
    inner_pos = jnp.arange(BLK, dtype=jnp.int32)
    causal = inner_pos[:, None] >= inner_pos[None, :]
    diagonal = jnp.arange(MAXA + 1, dtype=jnp.int32)[None, :, None] == MAXA
    allowed = jnp.where(diagonal, causal[:, None, :], is_live[None, :, None])
    return allowed.reshape(BLK, (MAXA + 1) * BLK)


def tile_backward(query_tile, grad_tile, table_rows, allowed):
    key_count = table_rows.shape[0]
    groups = query_tile.shape[1]
    score_scale = HD ** (-0.5)
    key_rows = table_rows[:, : groups * HD].reshape(key_count, groups, HD)
    value_rows = table_rows[:, groups * HD :].reshape(key_count, groups, HD)
    scores = (
        jnp.einsum("qghd,kgd->ghqk", query_tile, key_rows, preferred_element_type=jnp.float32)
        * score_scale
    )
    masked = jnp.where(allowed, scores, -jnp.inf)
    row_max = jnp.max(masked, axis=-1, keepdims=True)
    row_total = jnp.sum(jnp.where(allowed, jnp.exp(scores - row_max), 0.0), axis=-1, keepdims=True)
    log_total = row_max + jnp.log(row_total)
    weights = jnp.where(allowed, jnp.exp(scores - log_total), 0.0)
    dprobs = jnp.einsum("qghd,kgd->ghqk", grad_tile, value_rows, preferred_element_type=jnp.float32)
    row_delta = jnp.sum(weights * dprobs, axis=-1, keepdims=True)
    dscores = weights * (dprobs - row_delta)
    probs_low = weights.astype(jnp.bfloat16)
    dscores_low = dscores.astype(jnp.bfloat16)
    grad_query = (
        jnp.einsum("ghqk,kgd->qghd", dscores_low, key_rows, preferred_element_type=jnp.float32)
        * score_scale
    )
    grad_key = jnp.einsum(
        "ghqk,qghd->kgd", dscores_low, query_tile, preferred_element_type=jnp.float32
    )
    grad_value = jnp.einsum(
        "ghqk,qghd->kgd", probs_low, grad_tile, preferred_element_type=jnp.float32
    )
    both_grads = jnp.concatenate(
        [grad_key.reshape(key_count, groups * HD), grad_value.reshape(key_count, groups * HD)],
        axis=1,
    )
    return (grad_query.astype(jnp.bfloat16), both_grads)


def body(queries, keys, values, grad_out, ancestor_ids, ancestor_count):
    tok_rows = queries.shape[0]
    own_blocks = tok_rows // BLK
    groups = keys.shape[1] // HD
    pair_width = 2 * groups * HD
    first_block = lax.axis_index("ctx") * own_blocks
    pair_rows = jnp.concatenate([keys, values], axis=1)
    depth_range = jnp.arange(MAXA, dtype=jnp.int32)
    own_range = jnp.arange(own_blocks, dtype=jnp.int32)
    is_live = depth_range[None, :] < ancestor_count[:, None]
    gathered = lax.all_gather(pair_rows, "ctx", axis=0, tiled=True)
    kv_table = gathered.reshape(-1, BLK, pair_width)
    diagonal_rows = first_block + own_range
    row_lists = jnp.concatenate([ancestor_ids, diagonal_rows[:, None]], axis=1)
    live_lists = jnp.concatenate([is_live, jnp.ones((own_blocks, 1), jnp.int32) > 0], axis=1)
    query_tiles = queries.reshape(own_blocks, BLK, groups, HQ_KV, HD)
    grad_tiles = grad_out.reshape(own_blocks, BLK, groups, HQ_KV, HD)

    def visit(accum, packed):
        query_tile, grad_tile, tile_rows, tile_live = packed
        table_rows = jnp.take(kv_table, tile_rows, axis=0).reshape((MAXA + 1) * BLK, pair_width)
        grad_query, both_grads = tile_backward(
            query_tile, grad_tile, table_rows, tile_mask(tile_live)
        )
        accum = accum.at[tile_rows].add(both_grads.reshape(MAXA + 1, BLK, pair_width))
        return (accum, grad_query)

    initial = jnp.zeros(kv_table.shape, jnp.float32)
    accum, query_grads = lax.scan(visit, initial, (query_tiles, grad_tiles, row_lists, live_lists))
    flat_rows = lax.psum_scatter(
        accum.reshape(-1, pair_width), "ctx", scatter_dimension=0, tiled=True
    )
    score_scale = HD ** (-0.5)
    grad_queries = query_grads.reshape(tok_rows, groups * HQ_KV * HD)
    grad_keys = (flat_rows[:, : groups * HD] * score_scale).astype(jnp.bfloat16)
    grad_values = flat_rows[:, groups * HD :].astype(jnp.bfloat16)
    return (grad_queries, grad_keys, grad_values)


def solution(mesh):
    in_specs = (
        P(("rep", "ctx"), "head"),
        P(("rep", "ctx"), "head"),
        P(("rep", "ctx"), "head"),
        P(("rep", "ctx"), "head"),
        P(("rep", "ctx"), None),
        P(("rep", "ctx")),
    )
    out_specs = (P(("rep", "ctx"), "head"), P(("rep", "ctx"), "head"), P(("rep", "ctx"), "head"))
    return jax.shard_map(body, mesh=mesh, in_specs=in_specs, out_specs=out_specs, check_vma=False)
```

profile of v0, /device:TPU:1, one launch (start us, length us, event | category | flops | bytes accessed | tf_op | source)
XLA Modules:
  0.0 444.6 jit_solution(4026031871396907810)
XLA Ops:
  9.4 3.5 copy.40
  15.0 71.3 %all-gather.2.cloned.1.call-done = bf16[32768,256]{1,0:T(8,128)(2,1)} async-done(((bf16[1024,256]{1,0:T(8,128)(2,1)}), bf16[32768,256]{1,0:T(8,128)(2,1)}) %all-gather.2.cloned.1.call-update) | async-done | bytes 16777232 | tf_op jit(solution)/shard_map/all_gather | solution.py:67
  86.3 11.2 %broadcast_in_dim.86 = f32[256,128,256]{2,1,0:T(8,128)} broadcast(f32[]{:T(128)} %constant.27.clone.1), dimensions={} | broadcast | bytes 33554436 | tf_op jit(solution)/shard_map/broadcast_in_dim | solution.py:84
  97.5 173.2 %while.12 = (s32[]{:T(128)}, f32[256,128,256]{2,1,0:T(8,128)}, bf16[8,128,1,8,128]{4,3,1,0,2:T(8,128)(2,1)}, s32[8,7]{1,0:T(8,128)S(1)}, bf16[8,128,1,8,128]{4,3...) while((s32[]{:T(128)}, f32[256,128,256]{2,1,0:T(8,128)}, ...), condition=%wide.region_5.6_spmd, body=%wide.region_0.5_spmd.sunk | while | flops 1195670528 | bytes 74602112 | solution.py:85
  98.0 6.3 %gather_fusion = bf16[7,128,256]{2,1,0:T(8,128)(2,1)S(1)} fusion(bf16[256,128,256]{2,1,0:T(8,128)(2,1)} %get-tuple-element.169, s32[1024]{0:T(1024)S(1)} %pad_clamp_fusion.2), kind=kCustom, calls=%fused_computation.clone.1 | custom fusion | bytes 917532 | tf_op jit(solution)/shard_map/while/body/eval_jaxpr/jit(_take)/gather | solution.py:77
  109.2 3.3 fusion.45
  119.6 6.3 %gather_fusion = bf16[7,128,256]{2,1,0:T(8,128)(2,1)S(1)} fusion(bf16[256,128,256]{2,1,0:T(8,128)(2,1)} %get-tuple-element.169, s32[1024]{0:T(1024)S(1)} %pad_clamp_fusion.2), kind=kCustom, calls=%fused_computation.clone.1 | custom fusion | bytes 917532 | tf_op jit(solution)/shard_map/while/body/eval_jaxpr/jit(_take)/gather | solution.py:77
  130.8 3.3 fusion.45
  141.3 6.3 %gather_fusion = bf16[7,128,256]{2,1,0:T(8,128)(2,1)S(1)} fusion(bf16[256,128,256]{2,1,0:T(8,128)(2,1)} %get-tuple-element.169, s32[1024]{0:T(1024)S(1)} %pad_clamp_fusion.2), kind=kCustom, calls=%fused_computation.clone.1 | custom fusion | bytes 917532 | tf_op jit(solution)/shard_map/while/body/eval_jaxpr/jit(_take)/gather | solution.py:77
  152.5 3.3 fusion.45
  159.2 3.2 scatter_fusion
  163.0 6.3 %gather_fusion = bf16[7,128,256]{2,1,0:T(8,128)(2,1)S(1)} fusion(bf16[256,128,256]{2,1,0:T(8,128)(2,1)} %get-tuple-element.169, s32[1024]{0:T(1024)S(1)} %pad_clamp_fusion.2), kind=kCustom, calls=%fused_computation.clone.1 | custom fusion | bytes 917532 | tf_op jit(solution)/shard_map/while/body/eval_jaxpr/jit(_take)/gather | solution.py:77
  174.2 3.3 fusion.45
  184.6 6.3 %gather_fusion = bf16[7,128,256]{2,1,0:T(8,128)(2,1)S(1)} fusion(bf16[256,128,256]{2,1,0:T(8,128)(2,1)} %get-tuple-element.169, s32[1024]{0:T(1024)S(1)} %pad_clamp_fusion.2), kind=kCustom, calls=%fused_computation.clone.1 | custom fusion | bytes 917532 | tf_op jit(solution)/shard_map/while/body/eval_jaxpr/jit(_take)/gather | solution.py:77
  195.8 3.3 fusion.45
  206.2 6.3 %gather_fusion = bf16[7,128,256]{2,1,0:T(8,128)(2,1)S(1)} fusion(bf16[256,128,256]{2,1,0:T(8,128)(2,1)} %get-tuple-element.169, s32[1024]{0:T(1024)S(1)} %pad_clamp_fusion.2), kind=kCustom, calls=%fused_computation.clone.1 | custom fusion | bytes 917532 | tf_op jit(solution)/shard_map/while/body/eval_jaxpr/jit(_take)/gather | solution.py:77
  217.4 3.3 fusion.45
  224.1 3.3 scatter_fusion
  227.9 6.3 %gather_fusion = bf16[7,128,256]{2,1,0:T(8,128)(2,1)S(1)} fusion(bf16[256,128,256]{2,1,0:T(8,128)(2,1)} %get-tuple-element.169, s32[1024]{0:T(1024)S(1)} %pad_clamp_fusion.2), kind=kCustom, calls=%fused_computation.clone.1 | custom fusion | bytes 917532 | tf_op jit(solution)/shard_map/while/body/eval_jaxpr/jit(_take)/gather | solution.py:77
  239.1 3.3 fusion.45
  245.9 3.2 scatter_fusion
  249.6 6.3 %gather_fusion = bf16[7,128,256]{2,1,0:T(8,128)(2,1)S(1)} fusion(bf16[256,128,256]{2,1,0:T(8,128)(2,1)} %get-tuple-element.169, s32[1024]{0:T(1024)S(1)} %pad_clamp_fusion.2), kind=kCustom, calls=%fused_computation.clone.1 | custom fusion | bytes 917532 | tf_op jit(solution)/shard_map/while/body/eval_jaxpr/jit(_take)/gather | solution.py:77
  260.8 3.3 fusion.45
  274.2 159.9 %reduce-scatter.2.cloned.1.call-done = f32[1024,256]{1,0:T(8,128)} async-done(((f32[32768,256]{1,0:T(8,128)}), f32[1024,256]{1,0:T(8,128)}) %reduce-scatter.2.cloned.1.call-update) | async-done | bytes 1048592 | tf_op jit(solution)/shard_map/reduce_scatter | solution.py:86
  (243 shorter events, 96.6 us)
Async XLA Ops:
  7.2 5.7 %copy-start.2 = (bf16[1024,1024]{1,0:T(8,128)(2,1)S(1)}, bf16[1024,1024]{1,0:T(8,128)(2,1)}, u32[]{:S(2)}) copy-start(bf16[1024,1024]{1,0:T(8,128)(2,1)} %param.11) | copy-start | bytes 6291460
  7.2 79.1 %all-gather.2.cloned.1.call-start = ((), (), s32[]{:S(2)}) async-start(), calls=%async_computation.1 | async-start | bytes 17301504 | tf_op jit(solution)/shard_map/all_gather | solution.py:67
  9.3 424.9 %reduce-scatter.2.cloned.1.call-start = ((), (), s32[]{:S(2)}) async-start(), calls=%async_computation.2 | async-start | bytes 34603008 | tf_op jit(solution)/shard_map/reduce_scatter | solution.py:86
  9.3 5.5 %copy-start.5 = (s32[8]{0:T(128)S(1)}, s32[8]{0:T(128)}, u32[]{:S(2)}) copy-start(s32[8]{0:T(128)} %param.13) | copy-start | bytes 100
  9.4 5.6 %copy-start.4 = (s32[8,6]{1,0:T(8,128)S(1)}, s32[8,6]{1,0:T(8,128)}, u32[]{:S(2)}) copy-start(s32[8,6]{1,0:T(8,128)} %param.12) | copy-start | bytes 580
  106.3 1.8 copy-start
  109.2 3.3 copy-start.1
  127.9 1.8 copy-start
  130.8 3.3 copy-start.1
  149.5 1.8 copy-start
  152.4 3.3 copy-start.1
  171.2 1.8 copy-start
  174.1 3.3 copy-start.1
  192.8 1.8 copy-start
  195.8 3.3 copy-start.1
  214.5 1.8 copy-start
  217.4 3.3 copy-start.1
  236.2 1.8 copy-start
  239.1 3.3 copy-start.1
  257.9 1.8 copy-start
  260.8 3.3 copy-start.1
  270.7 1.6 copy-start.3
Sparse Core Ops, SparseCore 0:
  10.3 75.9 all-gather.1
  270.9 163.2 reduce-scatter.1
where the time goes:
time: 446 us; the launch traced here: 445 us
  waiting for transfers between devices  231 us (52%)
  local copies, waits for them, and re-layouts  101 us (23%)
  other arithmetic  48.7 us (11%)
  matrix products  48.2 us (11%)
  between operations  14.1 us (3%)
    reduce_scatter x1, waiting for transfers between devices, body(): lax.psum_scatter(accum.reshape(-1, pair_width), 'ctx', scatter_dimension=...  160 us
    all_gather x1, waiting for transfers between devices, body(): gathered = lax.all_gather(pair_rows, 'ctx', axis=0, tiled=True)  71.3 us
    gather x8, local copies, waits for them, and re-layouts, visit(): jnp.take(kv_table, tile_rows, axis=0).reshape((MAXA + 1) * BLK, pair_width)  50.8 us
    dot_general x8, matrix products, tile_backward(): jnp.einsum('qghd,kgd->ghqk', grad_tile, value_rows, preferred_element_typ...  26.3 us
    scatter-add x8, other arithmetic, visit(): accum.at[tile_rows].add(both_grads.reshape(MAXA + 1, BLK, pair_width))  25.5 us
    broadcast_in_dim x1, local copies, waits for them, and re-layouts, body(): initial = jnp.zeros(kv_table.shape, jnp.float32)  11.2 us
    unnamed x11, local copies, waits for them, and re-layouts  8.98 us
  transfers between devices with their start and end apart: 2, of which 2 were waited for; matrix products, arithmetic and copies ran while one was open for 2% of the time, Pallas kernels for 0%

commit v1 on v0

v1 whole, which is shorter than its diff:
```python
import functools

import jax
import jax.numpy as jnp
from jax import lax
from jax.experimental import pallas as pl
from jax.experimental.pallas import tpu as pltpu
from jax.sharding import PartitionSpec as P

HD = 128
HQ = 8
BLK = 128
MAXA = 6
OWN = 8
SHARDS = 32
ROWS = HQ * BLK
CHUNK = 256
PIECE = 8 * MAXA
MARK = 1e30
MARK_MIN = 1e29
SCALE = HD ** (-0.5)
LOG2E = 1.4426950408889634
MIB = 1024 * 1024

F32 = jnp.float32
BF16 = jnp.bfloat16


def last_of_depth(count_ref, depth):
    found = jnp.int32(-1)
    for b in range(OWN):
        found = jnp.where(count_ref[b] == depth, jnp.int32(b), found)
    return found


def pack_kernel(count_ref, k_ref, v_ref, out_ref):
    for half, ref in enumerate((k_ref, v_ref)):
        parts = []
        for j in range(MAXA):
            last = last_of_depth(count_ref, j)
            row = pl.multiple_of(jnp.maximum(last, 0) * BLK, BLK)
            block = ref[pl.ds(row, BLK), :].astype(F32)
            block = jnp.where(last >= 0, block, MARK)
            parts.append(block.reshape(16, 8, HD))
        out_ref[pl.ds(half * 16, 16)] = jnp.concatenate(parts, axis=1).astype(BF16)


def pack(keys, values, count):
    return pl.pallas_call(
        pack_kernel,
        out_shape=jax.ShapeDtypeStruct((SHARDS, PIECE, HD), BF16),
        in_specs=[
            pl.BlockSpec(memory_space=pltpu.SMEM),
            pl.BlockSpec(memory_space=pltpu.VMEM),
            pl.BlockSpec(memory_space=pltpu.VMEM),
        ],
        out_specs=pl.BlockSpec(memory_space=pltpu.VMEM),
        name="pack",
    )(count, keys, values)


def stack_kernel(in_ref, out_ref):
    held = jnp.full((PIECE, HD), MARK, F32)
    for t in range(SHARDS):
        out_ref[t] = held.astype(BF16)
        x = in_ref[t].astype(F32)
        held = jnp.where(x < MARK_MIN, x, held)


def stack(pieces):
    return pl.pallas_call(
        stack_kernel,
        out_shape=jax.ShapeDtypeStruct((SHARDS, PIECE, HD), BF16),
        in_specs=[pl.BlockSpec(memory_space=pltpu.VMEM)],
        out_specs=pl.BlockSpec(memory_space=pltpu.VMEM),
        name="stack",
    )(pieces)


def segsum_kernel(flag_ref, in_ref, out_ref):
    total = jnp.zeros((PIECE, HD), F32)
    for t in range(SHARDS - 1, -1, -1):
        here = flag_ref[t].astype(F32) < MARK_MIN
        out_ref[t] = jnp.where(here, total, 0.0).astype(BF16)
        total = jnp.where(here, 0.0, total) + in_ref[t].astype(F32)


def segsum(flags, pieces):
    return pl.pallas_call(
        segsum_kernel,
        out_shape=jax.ShapeDtypeStruct((SHARDS, PIECE, HD), BF16),
        in_specs=[pl.BlockSpec(memory_space=pltpu.VMEM)] * 2,
        out_specs=pl.BlockSpec(memory_space=pltpu.VMEM),
        name="segsum",
    )(flags, pieces)


def final_kernel(count_ref, dk_ref, dv_ref, in_ref, gk_ref, gv_ref, acc):
    for half, (ref, out, scale) in enumerate(((dk_ref, gk_ref, SCALE), (dv_ref, gv_ref, 1.0))):
        acc[...] = ref[...]
        piece = in_ref[pl.ds(half * 16, 16)].astype(F32)
        for j in range(MAXA):
            last = last_of_depth(count_ref, j)
            row = pl.multiple_of(jnp.maximum(last, 0) * BLK, BLK)
            term = piece[:, 8 * j : 8 * j + 8, :].reshape(BLK, HD)
            acc[pl.ds(row, BLK), :] += jnp.where(last >= 0, term, 0.0)
        out[...] = (acc[...] * scale).astype(BF16)


def final(count, dk, dv, pieces):
    shape = jax.ShapeDtypeStruct((OWN * BLK, HD), BF16)
    return pl.pallas_call(
        final_kernel,
        out_shape=(shape, shape),
        in_specs=[pl.BlockSpec(memory_space=pltpu.SMEM)] + [pl.BlockSpec(memory_space=pltpu.VMEM)] * 3,
        out_specs=[pl.BlockSpec(memory_space=pltpu.VMEM)] * 2,
        scratch_shapes=[pltpu.VMEM((OWN * BLK, HD), F32)],
        name="final",
    )(count, dk, dv, pieces)


def nt(a, b):
    return lax.dot_general(a, b, (((1,), (1,)), ((), ())), preferred_element_type=F32)


def nn(a, b):
    return lax.dot_general(a, b, (((1,), (0,)), ((), ())), preferred_element_type=F32)


def tn(a, b):
    return lax.dot_general(a, b, (((0,), (0,)), ((), ())), preferred_element_type=F32)


def attn_kernel(
    ids_ref,
    count_ref,
    base_ref,
    q_ref,
    o_ref,
    k_ref,
    v_ref,
    ext_ref,
    dq_ref,
    dk_ref,
    dv_ref,
    back_ref,
    kt,
    vt,
    dke,
    dve,
    qs,
    os,
    e_scr,
    d_scr,
    p_scr,
    s_scr,
    kb,
):
    b = pl.program_id(0)
    base = base_ref[0]

    @pl.when(b == 0)
    def _():
        kt[pl.ds(0, OWN * BLK), :] = k_ref[...]
        vt[pl.ds(0, OWN * BLK), :] = v_ref[...]
        for half, tab in enumerate((kt, vt)):
            piece = ext_ref[pl.ds(half * 16, 16)].astype(F32)
            for j in range(MAXA):
                rows = piece[:, 8 * j : 8 * j + 8, :].reshape(BLK, HD)
                tab[pl.ds((OWN + j) * BLK, BLK), :] = rows.astype(BF16)
        dke[...] = jnp.zeros_like(dke)
        dve[...] = jnp.zeros_like(dve)

    for h in range(HQ):
        qs[pl.ds(h * BLK, BLK), :] = q_ref[:, h * HD : (h + 1) * HD]
        os[pl.ds(h * BLK, BLK), :] = o_ref[:, h * HD : (h + 1) * HD]

    count = count_ref[b]
    coef = SCALE * LOG2E
    key_pos = lax.broadcasted_iota(jnp.int32, (BLK, CHUNK), 0)
    row_pos = lax.rem(lax.broadcasted_iota(jnp.int32, (BLK, CHUNK), 1), BLK)
    causal = key_pos <= row_pos

    def table_row(j):
        ident = ids_ref[b * MAXA + j]
        place = jnp.where(ident >= base, ident - base, OWN + j)
        return pl.multiple_of(place * BLK, BLK)

    for n in range(MAXA + 1):

        @pl.when(count == n)
        def _(n=n):
            places = [table_row(j) for j in range(n)] + [pl.multiple_of(b * BLK, BLK)]
            nk = (n + 1) * BLK
            for j in range(n + 1):
                kb[pl.ds(j * BLK, BLK), :] = kt[pl.ds(places[j], BLK), :]

            def visit(c, carry):
                start = pl.multiple_of(c * CHUNK, CHUNK)
                qc = qs[pl.ds(start, CHUNK), :]
                oc = os[pl.ds(start, CHUNK), :]
                tops, sums, dots = [], [], []
                for j in range(n + 1):
                    s = nt(kt[pl.ds(places[j], BLK), :], qc)
                    if j == n:
                        s = jnp.where(causal, s, -jnp.inf)
                    top = jnp.max(s, axis=0, keepdims=True)
                    e = jnp.exp2((s - top) * coef)
                    d = nt(vt[pl.ds(places[j], BLK), :], oc)
                    tops.append(top)
                    sums.append(jnp.sum(e, axis=0, keepdims=True))
                    dots.append(jnp.sum(e * d, axis=0, keepdims=True))
                    e_scr[pl.ds(j * BLK, BLK), :] = e
                    d_scr[pl.ds(j * BLK, BLK), :] = d
                top = functools.reduce(jnp.maximum, tops)
                factors = [jnp.exp2((t - top) * coef) for t in tops]
                total = sum(f * x for f, x in zip(factors, sums))
                inv = 1.0 / total
                delta = sum(f * x for f, x in zip(factors, dots)) * inv
                for j in range(n + 1):
                    p = e_scr[pl.ds(j * BLK, BLK), :] * (factors[j] * inv)
                    ds = p * (d_scr[pl.ds(j * BLK, BLK), :] - delta)
                    p_scr[pl.ds(j * BLK, BLK), pl.ds(start, CHUNK)] = p.astype(BF16)
                    s_scr[pl.ds(j * BLK, BLK), pl.ds(start, CHUNK)] = ds.astype(BF16)
                return carry

            lax.fori_loop(0, ROWS // CHUNK, visit, 0)
            dv = nn(p_scr[pl.ds(0, nk), :], os[...])
            dk = nn(s_scr[pl.ds(0, nk), :], qs[...])
            for j in range(n + 1):
                dke[pl.ds(places[j], BLK), :] += dk[j * BLK : (j + 1) * BLK]
                dve[pl.ds(places[j], BLK), :] += dv[j * BLK : (j + 1) * BLK]
            dq = tn(s_scr[pl.ds(0, nk), :], kb[pl.ds(0, nk), :]) * SCALE
            for h in range(HQ):
                dq_ref[:, h * HD : (h + 1) * HD] = dq[h * BLK : (h + 1) * BLK].astype(BF16)

    @pl.when(b == OWN - 1)
    def _():
        dk_ref[...] = dke[pl.ds(0, OWN * BLK), :]
        dv_ref[...] = dve[pl.ds(0, OWN * BLK), :]
        for half, acc in enumerate((dke, dve)):
            parts = [acc[pl.ds((OWN + j) * BLK, BLK), :].reshape(16, 8, HD) for j in range(MAXA)]
            back_ref[pl.ds(half * 16, 16)] = jnp.concatenate(parts, axis=1).astype(BF16)


def attention(ids, count, base, queries, grad_out, keys, values, ext):
    whole = lambda shape: pl.BlockSpec(shape, lambda b, *_: (0,) * len(shape))
    tiles = OWN + MAXA
    return pl.pallas_call(
        attn_kernel,
        grid_spec=pltpu.PrefetchScalarGridSpec(
            num_scalar_prefetch=3,
            grid=(OWN,),
            in_specs=[
                pl.BlockSpec((BLK, ROWS), lambda b, *_: (b, 0)),
                pl.BlockSpec((BLK, ROWS), lambda b, *_: (b, 0)),
                whole((OWN * BLK, HD)),
                whole((OWN * BLK, HD)),
                whole((SHARDS, PIECE, HD)),
            ],
            out_specs=[
                pl.BlockSpec((BLK, ROWS), lambda b, *_: (b, 0)),
                whole((OWN * BLK, HD)),
                whole((OWN * BLK, HD)),
                whole((SHARDS, PIECE, HD)),
            ],
            scratch_shapes=[
                pltpu.VMEM((tiles * BLK, HD), BF16),
                pltpu.VMEM((tiles * BLK, HD), BF16),
                pltpu.VMEM((tiles * BLK, HD), F32),
                pltpu.VMEM((tiles * BLK, HD), F32),
                pltpu.VMEM((ROWS, HD), BF16),
                pltpu.VMEM((ROWS, HD), BF16),
                pltpu.VMEM(((MAXA + 1) * BLK, CHUNK), F32),
                pltpu.VMEM(((MAXA + 1) * BLK, CHUNK), F32),
                pltpu.VMEM(((MAXA + 1) * BLK, ROWS), BF16),
                pltpu.VMEM(((MAXA + 1) * BLK, ROWS), BF16),
                pltpu.VMEM(((MAXA + 1) * BLK, HD), BF16),
            ],
        ),
        out_shape=(
            jax.ShapeDtypeStruct((OWN * BLK, ROWS), BF16),
            jax.ShapeDtypeStruct((OWN * BLK, HD), F32),
            jax.ShapeDtypeStruct((OWN * BLK, HD), F32),
            jax.ShapeDtypeStruct((SHARDS, PIECE, HD), BF16),
        ),
        compiler_params=pltpu.CompilerParams(vmem_limit_bytes=48 * MIB),
        name="attention",
    )(ids, count, base, queries, grad_out, keys, values, ext)


def body(queries, keys, values, grad_out, ancestor_ids, ancestor_count):
    base = (lax.axis_index("ctx") * OWN).astype(jnp.int32).reshape(1)
    mine = pack(keys, values, ancestor_count)
    pieces = lax.all_to_all(mine, "ctx", 0, 0, tiled=True)
    ext = lax.all_to_all(stack(pieces), "ctx", 0, 0, tiled=True)
    grad_queries, dk, dv, back = attention(
        ancestor_ids.reshape(-1), ancestor_count, base, queries, grad_out, keys, values, ext
    )
    sums = segsum(pieces, lax.all_to_all(back, "ctx", 0, 0, tiled=True))
    terms = lax.all_to_all(sums, "ctx", 0, 0, tiled=True)
    grad_keys, grad_values = final(ancestor_count, dk, dv, terms)
    return (grad_queries, grad_keys, grad_values)


def solution(mesh):
    rows = P(("rep", "ctx"), "head")
    in_specs = (rows, rows, rows, rows, P(("rep", "ctx"), None), P(("rep", "ctx")))
    return jax.shard_map(
        body, mesh=mesh, in_specs=in_specs, out_specs=(rows, rows, rows), check_vma=False
    )
```

time: 446 us -> 108 us (0.24)
  waiting for transfers between devices: 231 us -> 10.2 us
  local copies, waits for them, and re-layouts: 101 us -> 1.67 us
  blocking collectives: 0 us -> 55.7 us
  other arithmetic: 48.7 us -> 0 us
  matrix products: 48.2 us -> 0 us
  Pallas kernels: 0 us -> 36.2 us
  between operations: 14.1 us -> 0.71 us
    reduce_scatter x1 -> x0, waiting for transfers between devices: 160 us -> none  [body(): lax.psum_scatter(accum.reshape(-1, pair_width), 'ctx', scatter_dimension=...]
    all_gather x1 -> x0, waiting for transfers between devices: 71.3 us -> none  [body(): gathered = lax.all_gather(pair_rows, 'ctx', axis=0, tiled=True)]
    all_to_all x0 -> x3, blocking collectives: none -> 55.7 us  [the longest x1 22 us: body(): sums = segsum(pieces, lax.all_to_all(back, 'ctx', 0, 0, tiled=True))]
    gather x8 -> x0, local copies, waits for them, and re-layouts: 50.8 us -> none  [visit(): jnp.take(kv_table, tile_rows, axis=0).reshape((MAXA + 1) * BLK, pair_width)]
    dot_general x40 -> x0, matrix products: 48.2 us -> none  [the longest x8 26.3 us: tile_backward(): jnp.einsum('qghd,kgd->ghqk', grad_tile, value_rows, preferred_element_typ...]
    pallas_call x0 -> x5, Pallas kernels: none -> 36.2 us  [the longest x1 28.1 us: attention(): pl.pallas_call(attn_kernel, grid_spec=pltpu.PrefetchScalarGridSpec(num_sc...]
    scatter-add x8 -> x0, other arithmetic: 25.5 us -> none  [visit(): accum.at[tile_rows].add(both_grads.reshape(MAXA + 1, BLK, pair_width))]
    broadcast_in_dim x25 -> x0, local copies, waits for them, and re-layouts: 12.4 us -> none  [the longest x1 11.2 us: body(): initial = jnp.zeros(kv_table.shape, jnp.float32)]
  transfers between devices with their start and end apart: 2 -> 1, of which waited for: 2 -> 1; matrix products, arithmetic and copies ran while one was open for 2% -> 0% of each run, Pallas kernels for 0% -> 0%
where the time goes in v1:
time: 108 us
  blocking collectives  55.7 us (52%)
  Pallas kernels  36.2 us (34%)
  waiting for transfers between devices  10.2 us (9%)
  starting transfers between devices  3.9 us (4%)
  local copies, waits for them, and re-layouts  1.67 us (2%)
    pallas_call x1, Pallas kernels, attention(): pl.pallas_call(attn_kernel, grid_spec=pltpu.PrefetchScalarGridSpec(num_sc...  28.1 us
    all_to_all x1, blocking collectives, body(): sums = segsum(pieces, lax.all_to_all(back, 'ctx', 0, 0, tiled=True))  22 us
    all_to_all x1, blocking collectives, body(): pieces = lax.all_to_all(mine, 'ctx', 0, 0, tiled=True)  18.9 us
    all_to_all x1, blocking collectives, body(): terms = lax.all_to_all(sums, 'ctx', 0, 0, tiled=True)  14.9 us
    all_to_all x1, waiting for transfers between devices, body(): ext = lax.all_to_all(stack(pieces), 'ctx', 0, 0, tiled=True)  10.2 us
    all_to_all x1, starting transfers between devices, body(): ext = lax.all_to_all(stack(pieces), 'ctx', 0, 0, tiled=True)  3.9 us
    pallas_call x1, Pallas kernels, final(): pl.pallas_call(final_kernel, out_shape=(shape, shape), in_specs=[pl.Block...  2.27 us
  transfers between devices with their start and end apart: 1, of which 1 were waited for; matrix products, arithmetic and copies ran while one was open for 0% of the time, Pallas kernels for 0%

profile of v1, /device:TPU:1, one launch (start us, length us, event | category | flops | bytes accessed | tf_op | source)
XLA Modules:
  0.0 108.4 jit_solution(2310631184046697768)
XLA Ops:
  0.6 0.0 copy-start.5
  0.6 0.0 copy-start.2
  0.7 0.0 copy-start.1
  0.7 0.0 copy-start.6
  0.7 0.0 copy-start
  0.7 2.0 %pack.1 = bf16[32,48,128]{2,1,0:T(8,128)(2,1)} custom-call(s32[8]{0:T(128)} %count_ref.5, bf16[1024,128]{1,0:T(8,128)(2,1)} %k_ref.3, bf16[1024,128]{1,0:T(8,128)(2,1)} %v_ref.3), custom_call_target="tpu_custom_call" | custom-call | tf_op jit(solution)/shard_map/pack/pallas_call | solution.py:49
  2.7 18.9 %all_to_all.20.in_ref.flag_ref = bf16[32,48,128]{2,1,0:T(8,128)(2,1)} all-to-all(bf16[32,48,128]{2,1,0:T(8,128)(2,1)} %pack.1), channel_id=1, replica_groups=mesh['ctx'=32,'head'=4,'rep'=1] {'ctx'}, dimensions={0} | all-to-all | bytes 786432 | tf_op jit(solution)/shard_map/all_to_all | solution.py:295
  21.6 1.8 %stack.1 = bf16[32,48,128]{2,1,0:T(8,128)(2,1)} custom-call(bf16[32,48,128]{2,1,0:T(8,128)(2,1)} %all_to_all.20.in_ref.flag_ref), custom_call_target="tpu_custom_call" | custom-call | tf_op jit(solution)/shard_map/stack/pallas_call | solution.py:71
  23.4 3.9 %all-to-all-start.1 = ((bf16[32,48,128]{2,1,0:T(8,128)(2,1)}), bf16[32,48,128]{2,1,0:T(8,128)(2,1)S(1)}, u32[]{:S(2)}, u32[]{:S(2)}) async-start(bf16[32,48,128]{2,1,0:T(8,128)(2,1)} %stack.1), calls=%async_computation.1 | async-start | bytes 786432 | tf_op jit(solution)/shard_map/all_to_all | solution.py:296
  27.3 0.0 copy-done.6
  27.3 0.1 reshape.12.ids_ref
  27.4 10.2 %all-to-all-done.1.ext_ref = bf16[32,48,128]{2,1,0:T(8,128)(2,1)S(1)} async-done(((bf16[32,48,128]{2,1,0:T(8,128)(2,1)}), bf16[32,48,128]{2,1,0:T(8,128)(2,1)S(1)}, u32[]{:S(2)}, u32[]{:S(2)}) %all-to-all-start.1) | async-done | bytes 393248 | tf_op jit(solution)/shard_map/all_to_all | solution.py:296
  37.6 0.0 copy-done.5
  37.6 0.0 copy-done.2
  37.6 0.0 copy-done.1
  37.6 0.0 copy-done
  37.6 28.1 %attention.1 = (bf16[1024,1024]{1,0:T(8,128)(2,1)}, f32[1024,128]{1,0:T(8,128)S(1)}, f32[1024,128]{1,0:T(8,128)S(1)}, bf16[32,48,128]{2,1,0:T(8,128)(2,1)S(1)}) custom-call(s32[48]{0:T(128)S(1)} %reshape.12.ids_ref, s32[8]{0:T(128)S(1)} %copy-done.5, s32[1]{0:T(128)} %bitcast.base_ref, bf16[1024,1024]{1,0:T(8,128)(2,1)S(1)} %copy-done, ...), custom_call_target="tpu_custom_call" | custom-call | tf_op jit(solution)/shard_map/attention/pallas_call | solution.py:249
  65.7 0.0 copy-start.3
  65.7 0.8 copy-done.3
  66.5 0.8 copy-done.4
  67.3 22.0 %all_to_all.21.in_ref = bf16[32,48,128]{2,1,0:T(8,128)(2,1)} all-to-all(bf16[32,48,128]{2,1,0:T(8,128)(2,1)S(1)} %get-tuple-element.12), channel_id=1, replica_groups=mesh['ctx'=32,'head'=4,'rep'=1] {'ctx'}, dimensions={0} | all-to-all | bytes 786432 | tf_op jit(solution)/shard_map/all_to_all | solution.py:300
  89.2 2.0 %segsum.1 = bf16[32,48,128]{2,1,0:T(8,128)(2,1)} custom-call(bf16[32,48,128]{2,1,0:T(8,128)(2,1)} %all_to_all.20.in_ref.flag_ref, bf16[32,48,128]{2,1,0:T(8,128)(2,1)} %all_to_all.21.in_ref), custom_call_target="tpu_custom_call" | custom-call | tf_op jit(solution)/shard_map/segsum/pallas_call | solution.py:89
  91.3 14.9 %all_to_all.22.in_ref = bf16[32,48,128]{2,1,0:T(8,128)(2,1)} all-to-all(bf16[32,48,128]{2,1,0:T(8,128)(2,1)} %segsum.1), channel_id=1, replica_groups=mesh['ctx'=32,'head'=4,'rep'=1] {'ctx'}, dimensions={0} | all-to-all | bytes 786432 | tf_op jit(solution)/shard_map/all_to_all | solution.py:301
  106.1 2.3 %final.1 = (bf16[1024,128]{1,0:T(8,128)(2,1)}, bf16[1024,128]{1,0:T(8,128)(2,1)}) custom-call(s32[8]{0:T(128)} %count_ref.5, f32[1024,128]{1,0:T(8,128)} %copy-done.3, f32[1024,128]{1,0:T(8,128)} %copy-done.4, bf16[32,48,128]{2,1,0:T(8,128)(2,1)} %all_to_all.22.in_ref), custom_call_target="tpu_custom_call" | custom-call | tf_op jit(solution)/shard_map/final/pallas_call | solution.py:112
  (1 shorter events, 0.0 us)
Async XLA Ops:
  0.6 37.0 %copy-start.5 = (s32[8]{0:T(128)S(1)}, s32[8]{0:T(128)}, u32[]{:S(2)}) copy-start(s32[8]{0:T(128)} %count_ref.5) | copy-start | bytes 100
  0.6 37.0 %copy-start.2 = (bf16[1024,128]{1,0:T(8,128)(2,1)S(1)}, bf16[1024,128]{1,0:T(8,128)(2,1)}, u32[]{:S(2)}) copy-start(bf16[1024,128]{1,0:T(8,128)(2,1)} %v_ref.3) | copy-start | bytes 786436
  0.7 37.0 %copy-start.1 = (bf16[1024,128]{1,0:T(8,128)(2,1)S(1)}, bf16[1024,128]{1,0:T(8,128)(2,1)}, u32[]{:S(2)}) copy-start(bf16[1024,128]{1,0:T(8,128)(2,1)} %k_ref.3) | copy-start | bytes 786436
  0.7 26.7 %copy-start.6 = (s32[8,6]{1,0:T(8,128)S(1)}, s32[8,6]{1,0:T(8,128)}, u32[]{:S(2)}) copy-start(s32[8,6]{1,0:T(8,128)} %param.10) | copy-start | bytes 580
  0.7 36.9 %copy-start = (bf16[1024,1024]{1,0:T(8,128)(2,1)S(1)}, bf16[1024,1024]{1,0:T(8,128)(2,1)}, u32[]{:S(2)}) copy-start(bf16[1024,1024]{1,0:T(8,128)(2,1)} %q_ref.1) | copy-start | bytes 6291460
  23.4 14.2 %all-to-all-start.1 = ((bf16[32,48,128]{2,1,0:T(8,128)(2,1)}), bf16[32,48,128]{2,1,0:T(8,128)(2,1)S(1)}, u32[]{:S(2)}, u32[]{:S(2)}) async-start(bf16[32,48,128]{2,1,0:T(8,128)(2,1)} %stack.1), calls=%async_computation.1 | async-start | bytes 786432 | tf_op jit(solution)/shard_map/all_to_all | solution.py:296
  65.7 0.8 copy-start.3
  66.5 0.8 copy-start.4

commit v2 on v1

--- a/solution.py
+++ b/solution.py
@@ -55,6 +55,7 @@
             pl.BlockSpec(memory_space=pltpu.VMEM),
         ],
         out_specs=pl.BlockSpec(memory_space=pltpu.VMEM),
+        compiler_params=pltpu.CompilerParams(vmem_limit_bytes=8 * MIB),
         name="pack",
     )(count, keys, values)
 
@@ -73,6 +74,7 @@
         out_shape=jax.ShapeDtypeStruct((SHARDS, PIECE, HD), BF16),
         in_specs=[pl.BlockSpec(memory_space=pltpu.VMEM)],
         out_specs=pl.BlockSpec(memory_space=pltpu.VMEM),
+        compiler_params=pltpu.CompilerParams(vmem_limit_bytes=8 * MIB),
         name="stack",
     )(pieces)
 
@@ -91,6 +93,7 @@
         out_shape=jax.ShapeDtypeStruct((SHARDS, PIECE, HD), BF16),
         in_specs=[pl.BlockSpec(memory_space=pltpu.VMEM)] * 2,
         out_specs=pl.BlockSpec(memory_space=pltpu.VMEM),
+        compiler_params=pltpu.CompilerParams(vmem_limit_bytes=8 * MIB),
         name="segsum",
     )(flags, pieces)
 
@@ -115,6 +118,7 @@
         in_specs=[pl.BlockSpec(memory_space=pltpu.SMEM)] + [pl.BlockSpec(memory_space=pltpu.VMEM)] * 3,
         out_specs=[pl.BlockSpec(memory_space=pltpu.VMEM)] * 2,
         scratch_shapes=[pltpu.VMEM((OWN * BLK, HD), F32)],
+        compiler_params=pltpu.CompilerParams(vmem_limit_bytes=8 * MIB),
         name="final",
     )(count, dk, dv, pieces)
 
@@ -148,13 +152,11 @@
     vt,
     dke,
     dve,
-    qs,
-    os,
-    e_scr,
-    d_scr,
-    p_scr,
-    s_scr,
     kb,
+    vb,
+    dka,
+    dva,
+    *slots,
 ):
     b = pl.program_id(0)
     base = base_ref[0]
@@ -171,12 +173,9 @@
         dke[...] = jnp.zeros_like(dke)
         dve[...] = jnp.zeros_like(dve)
 
-    for h in range(HQ):
-        qs[pl.ds(h * BLK, BLK), :] = q_ref[:, h * HD : (h + 1) * HD]
-        os[pl.ds(h * BLK, BLK), :] = o_ref[:, h * HD : (h + 1) * HD]
-
     count = count_ref[b]
     coef = SCALE * LOG2E
+    heads = CHUNK // HD
     key_pos = lax.broadcasted_iota(jnp.int32, (BLK, CHUNK), 0)
     row_pos = lax.rem(lax.broadcasted_iota(jnp.int32, (BLK, CHUNK), 1), BLK)
     causal = key_pos <= row_pos
@@ -186,53 +185,79 @@
         place = jnp.where(ident >= base, ident - base, OWN + j)
         return pl.multiple_of(place * BLK, BLK)
 
+    def rows_of(ref, c):
+        return jnp.concatenate(
+            [ref[:, c * CHUNK + h * HD : c * CHUNK + (h + 1) * HD] for h in range(heads)], axis=0
+        )
+
+    def first(n, c):
+        e_scr, d_scr, g_scr = slots[3 * (c % 2) : 3 * (c % 2) + 3]
+        nk = (n + 1) * BLK
+        s_all = nt(kb[pl.ds(0, nk), :], rows_of(q_ref, c))
+        d_all = nt(vb[pl.ds(0, nk), :], rows_of(o_ref, c))
+        tops, sums, dots = [], [], []
+        for j in range(n + 1):
+            s = s_all[j * BLK : (j + 1) * BLK]
+            d = d_all[j * BLK : (j + 1) * BLK]
+            if j == n:
+                s = jnp.where(causal, s, -jnp.inf)
+            top = jnp.max(s, axis=0, keepdims=True)
+            e = jnp.exp2((s - top) * coef)
+            tops.append(top)
+            sums.append(jnp.sum(e, axis=0, keepdims=True))
+            dots.append(jnp.sum(e * d, axis=0, keepdims=True))
+            e_scr[pl.ds(j * BLK, BLK), :] = e
+            d_scr[pl.ds(j * BLK, BLK), :] = d
+        top = functools.reduce(jnp.maximum, tops)
+        factors = [jnp.exp2((t - top) * coef) for t in tops]
+        inv = 1.0 / sum(f * x for f, x in zip(factors, sums))
+        delta = sum(f * x for f, x in zip(factors, dots)) * inv
+        for j in range(n + 1):
+            g_scr[j : j + 1, :] = factors[j] * inv
+        g_scr[MAXA + 1 : MAXA + 2, :] = delta
+
+    def second(n, c):
+        e_scr, d_scr, g_scr = slots[3 * (c % 2) : 3 * (c % 2) + 3]
+        nk = (n + 1) * BLK
+        delta = g_scr[MAXA + 1 : MAXA + 2, :]
+        ps, dss = [], []
+        for j in range(n + 1):
+            p = e_scr[pl.ds(j * BLK, BLK), :] * g_scr[j : j + 1, :]
+            ds = p * (d_scr[pl.ds(j * BLK, BLK), :] - delta)
+            ps.append(p.astype(BF16))
+            dss.append(ds.astype(BF16))
+        p_all = jnp.concatenate(ps, axis=0)
+        ds_all = jnp.concatenate(dss, axis=0)
+        dv = nn(p_all, rows_of(o_ref, c))
+        dk = nn(ds_all, rows_of(q_ref, c))
+        if c == 0:
+            dva[pl.ds(0, nk), :] = dv
+            dka[pl.ds(0, nk), :] = dk
+        else:
+            dva[pl.ds(0, nk), :] += dv
+            dka[pl.ds(0, nk), :] += dk
+        g = tn(kb[pl.ds(0, nk), :], ds_all) * SCALE
+        for h in range(heads):
+            at = c * CHUNK + h * HD
+            dq_ref[:, at : at + HD] = g[:, h * HD : (h + 1) * HD].T.astype(BF16)
+
     for n in range(MAXA + 1):
 
         @pl.when(count == n)
         def _(n=n):
             places = [table_row(j) for j in range(n)] + [pl.multiple_of(b * BLK, BLK)]
-            nk = (n + 1) * BLK
             for j in range(n + 1):
                 kb[pl.ds(j * BLK, BLK), :] = kt[pl.ds(places[j], BLK), :]
-
-            def visit(c, carry):
-                start = pl.multiple_of(c * CHUNK, CHUNK)
-                qc = qs[pl.ds(start, CHUNK), :]
-                oc = os[pl.ds(start, CHUNK), :]
-                tops, sums, dots = [], [], []
-                for j in range(n + 1):
-                    s = nt(kt[pl.ds(places[j], BLK), :], qc)
-                    if j == n:
-                        s = jnp.where(causal, s, -jnp.inf)
-                    top = jnp.max(s, axis=0, keepdims=True)
-                    e = jnp.exp2((s - top) * coef)
-                    d = nt(vt[pl.ds(places[j], BLK), :], oc)
-                    tops.append(top)
-                    sums.append(jnp.sum(e, axis=0, keepdims=True))
-                    dots.append(jnp.sum(e * d, axis=0, keepdims=True))
-                    e_scr[pl.ds(j * BLK, BLK), :] = e
-                    d_scr[pl.ds(j * BLK, BLK), :] = d
-                top = functools.reduce(jnp.maximum, tops)
-                factors = [jnp.exp2((t - top) * coef) for t in tops]
-                total = sum(f * x for f, x in zip(factors, sums))
-                inv = 1.0 / total
-                delta = sum(f * x for f, x in zip(factors, dots)) * inv
-                for j in range(n + 1):
-                    p = e_scr[pl.ds(j * BLK, BLK), :] * (factors[j] * inv)
-                    ds = p * (d_scr[pl.ds(j * BLK, BLK), :] - delta)
-                    p_scr[pl.ds(j * BLK, BLK), pl.ds(start, CHUNK)] = p.astype(BF16)
-                    s_scr[pl.ds(j * BLK, BLK), pl.ds(start, CHUNK)] = ds.astype(BF16)
-                return carry
-
-            lax.fori_loop(0, ROWS // CHUNK, visit, 0)
-            dv = nn(p_scr[pl.ds(0, nk), :], os[...])
-            dk = nn(s_scr[pl.ds(0, nk), :], qs[...])
+                vb[pl.ds(j * BLK, BLK), :] = vt[pl.ds(places[j], BLK), :]
+            chunks = ROWS // CHUNK
+            first(n, 0)
+            for c in range(chunks):
+                if c + 1 < chunks:
+                    first(n, c + 1)
+                second(n, c)
             for j in range(n + 1):
-                dke[pl.ds(places[j], BLK), :] += dk[j * BLK : (j + 1) * BLK]
-                dve[pl.ds(places[j], BLK), :] += dv[j * BLK : (j + 1) * BLK]
-            dq = tn(s_scr[pl.ds(0, nk), :], kb[pl.ds(0, nk), :]) * SCALE
-            for h in range(HQ):
-                dq_ref[:, h * HD : (h + 1) * HD] = dq[h * BLK : (h + 1) * BLK].astype(BF16)
+                dke[pl.ds(places[j], BLK), :] += dka[pl.ds(j * BLK, BLK), :]
+                dve[pl.ds(places[j], BLK), :] += dva[pl.ds(j * BLK, BLK), :]
 
     @pl.when(b == OWN - 1)
     def _():
@@ -269,14 +294,17 @@
                 pltpu.VMEM((tiles * BLK, HD), BF16),
                 pltpu.VMEM((tiles * BLK, HD), F32),
                 pltpu.VMEM((tiles * BLK, HD), F32),
-                pltpu.VMEM((ROWS, HD), BF16),
-                pltpu.VMEM((ROWS, HD), BF16),
+                pltpu.VMEM(((MAXA + 1) * BLK, HD), BF16),
+                pltpu.VMEM(((MAXA + 1) * BLK, HD), BF16),
+                pltpu.VMEM(((MAXA + 1) * BLK, HD), F32),
+                pltpu.VMEM(((MAXA + 1) * BLK, HD), F32),
+            ]
+            + [
                 pltpu.VMEM(((MAXA + 1) * BLK, CHUNK), F32),
                 pltpu.VMEM(((MAXA + 1) * BLK, CHUNK), F32),
-                pltpu.VMEM(((MAXA + 1) * BLK, ROWS), BF16),
-                pltpu.VMEM(((MAXA + 1) * BLK, ROWS), BF16),
-                pltpu.VMEM(((MAXA + 1) * BLK, HD), BF16),
-            ],
+                pltpu.VMEM((8, CHUNK), F32),
+            ]
+            * 2,
         ),
         out_shape=(
             jax.ShapeDtypeStruct((OWN * BLK, ROWS), BF16),

time: 108 us -> 91.5 us (0.85)
  Pallas kernels: 36.2 us -> 21 us
  blocking collectives: 55.7 us -> 53.9 us
    pallas_call x1, Pallas kernels: 28.1 us -> 17.9 us  [attention(): pl.pallas_call(attn_kernel, grid_spec=pltpu.PrefetchScalarGridSpec(num_sc...]
    pallas_call x1, Pallas kernels: 2.04 us -> 0.16 us  [segsum(): pl.pallas_call(segsum_kernel, out_shape=jax.ShapeDtypeStruct((SHARDS, PIE...]
    pallas_call x1, Pallas kernels: 2.02 us -> 0.63 us  [pack(): pl.pallas_call(pack_kernel, out_shape=jax.ShapeDtypeStruct((SHARDS, PIECE...]
    all_to_all x1, blocking collectives: 14.9 us -> 13.8 us  [body(): terms = lax.all_to_all(sums, 'ctx', 0, 0, tiled=True)]
    unnamed x14 -> x16, local copies, waits for them, and re-layouts: 1.59 us -> 2.57 us
where the time goes in v2:
time: 91.5 us; the launch traced here: 92.4 us
  blocking collectives  53.9 us (59%)
  Pallas kernels  21 us (23%)
  waiting for transfers between devices  10.2 us (11%)
  starting transfers between devices  3.9 us (4%)
  local copies, waits for them, and re-layouts  2.65 us (3%)
    all_to_all x1, blocking collectives, body(): sums = segsum(pieces, lax.all_to_all(back, 'ctx', 0, 0, tiled=True))  21.5 us
    all_to_all x1, blocking collectives, body(): pieces = lax.all_to_all(mine, 'ctx', 0, 0, tiled=True)  18.7 us
    pallas_call x1, Pallas kernels, attention(): pl.pallas_call(attn_kernel, grid_spec=pltpu.PrefetchScalarGridSpec(num_sc...  17.9 us
    all_to_all x1, blocking collectives, body(): terms = lax.all_to_all(sums, 'ctx', 0, 0, tiled=True)  13.8 us
    all_to_all x1, waiting for transfers between devices, body(): ext = lax.all_to_all(stack(pieces), 'ctx', 0, 0, tiled=True)  10.2 us
    all_to_all x1, starting transfers between devices, body(): ext = lax.all_to_all(stack(pieces), 'ctx', 0, 0, tiled=True)  3.9 us
    unnamed x16, local copies, waits for them, and re-layouts  2.57 us
  transfers between devices with their start and end apart: 1, of which 1 were waited for; matrix products, arithmetic and copies ran while one was open for 0% of the time, Pallas kernels for 0%

profile of v2, /device:TPU:1, one launch (start us, length us, event | category | flops | bytes accessed | tf_op | source)
XLA Modules:
  0.0 92.4 jit_solution(16777197304336686452)
XLA Ops:
  0.6 0.0 copy-start.1
  0.6 0.9 %copy-done.1 = bf16[1024,128]{1,0:T(8,128)(2,1)S(1)} copy-done((bf16[1024,128]{1,0:T(8,128)(2,1)S(1)}, bf16[1024,128]{1,0:T(8,128)(2,1)}, u32[]{:S(2)}) %copy-start.1) | copy-done | bytes 262168
  1.6 0.0 copy-start.3
  1.6 0.9 %copy-done.3 = bf16[1024,128]{1,0:T(8,128)(2,1)S(1)} copy-done((bf16[1024,128]{1,0:T(8,128)(2,1)S(1)}, bf16[1024,128]{1,0:T(8,128)(2,1)}, u32[]{:S(2)}) %copy-start.3) | copy-done | bytes 262168
  2.5 0.0 copy-start.5
  2.5 0.7 copy-done.5
  3.2 0.0 copy-start.7
  3.2 0.0 copy-start.6
  3.2 0.6 pack.1
  3.8 18.7 %all_to_all.20.in_ref.flag_ref = bf16[32,48,128]{2,1,0:T(8,128)(2,1)S(1)} all-to-all(bf16[32,48,128]{2,1,0:T(8,128)(2,1)S(1)} %pack.1), channel_id=1, replica_groups=mesh['ctx'=32,'head'=4,'rep'=1] {'ctx'}, dimensions={0} | all-to-all | bytes 786432 | tf_op jit(solution)/shard_map/all_to_all | solution.py:323
  22.5 0.8 stack.1
  23.4 3.9 %all-to-all-start.1 = ((bf16[32,48,128]{2,1,0:T(8,128)(2,1)}), bf16[32,48,128]{2,1,0:T(8,128)(2,1)S(1)}, u32[]{:S(2)}, u32[]{:S(2)}) async-start(bf16[32,48,128]{2,1,0:T(8,128)(2,1)} %stack.1), calls=%async_computation.1 | async-start | bytes 786432 | tf_op jit(solution)/shard_map/all_to_all | solution.py:324
  27.3 0.0 copy-done.7
  27.3 0.1 reshape.12.ids_ref
  27.4 10.2 %all-to-all-done.1.ext_ref = bf16[32,48,128]{2,1,0:T(8,128)(2,1)S(1)} async-done(((bf16[32,48,128]{2,1,0:T(8,128)(2,1)}), bf16[32,48,128]{2,1,0:T(8,128)(2,1)S(1)}, u32[]{:S(2)}, u32[]{:S(2)}) %all-to-all-start.1) | async-done | bytes 393248 | tf_op jit(solution)/shard_map/all_to_all | solution.py:324
  37.6 0.0 copy-done
  37.6 0.0 copy-done.2
  37.6 0.0 copy-done.4
  37.6 0.0 copy-done.6
  37.6 17.9 %attention.1 = (bf16[1024,1024]{1,0:T(8,128)(2,1)}, f32[1024,128]{1,0:T(8,128)S(1)}, f32[1024,128]{1,0:T(8,128)S(1)}, bf16[32,48,128]{2,1,0:T(8,128)(2,1)S(1)}) custom-call(s32[48]{0:T(128)S(1)} %reshape.12.ids_ref, s32[8]{0:T(128)S(1)} %copy-done.6, s32[1]{0:T(128)} %bitcast.base_ref, bf16[1024,1024]{1,0:T(8,128)(2,1)S(1)} %copy-done, ...), custom_call_target="tpu_custom_call" | custom-call | tf_op jit(solution)/shard_map/attention/pallas_call | solution.py:274
  55.5 21.5 %all_to_all.21.in_ref = bf16[32,48,128]{2,1,0:T(8,128)(2,1)S(1)} all-to-all(bf16[32,48,128]{2,1,0:T(8,128)(2,1)S(1)} %get-tuple-element.12), channel_id=1, replica_groups=mesh['ctx'=32,'head'=4,'rep'=1] {'ctx'}, dimensions={0} | all-to-all | bytes 786432 | tf_op jit(solution)/shard_map/all_to_all | solution.py:328
  76.9 0.2 segsum.1
  77.1 13.8 %all_to_all.22.in_ref = bf16[32,48,128]{2,1,0:T(8,128)(2,1)S(1)} all-to-all(bf16[32,48,128]{2,1,0:T(8,128)(2,1)S(1)} %segsum.1), channel_id=1, replica_groups=mesh['ctx'=32,'head'=4,'rep'=1] {'ctx'}, dimensions={0} | all-to-all | bytes 786432 | tf_op jit(solution)/shard_map/all_to_all | solution.py:329
  90.8 1.5 %final.1 = (bf16[1024,128]{1,0:T(8,128)(2,1)}, bf16[1024,128]{1,0:T(8,128)(2,1)}) custom-call(s32[8]{0:T(128)S(1)} %copy-done.6, f32[1024,128]{1,0:T(8,128)S(1)} %get-tuple-element.10.dk_ref, f32[1024,128]{1,0:T(8,128)S(1)} %get-tuple-element.11.dv_ref, bf16[32,48,128]{2,1,0:T(8,128)(2,1)S(1)} %all_to_all.22.in_ref), custom_call_target="tpu_custom_call" | custom-call | tf_op jit(solution)/shard_map/final/pallas_call | solution.py:115
  (3 shorter events, 0.0 us)
Async XLA Ops:
  0.6 1.0 %copy-start.1 = (bf16[1024,128]{1,0:T(8,128)(2,1)S(1)}, bf16[1024,128]{1,0:T(8,128)(2,1)}, u32[]{:S(2)}) copy-start(bf16[1024,128]{1,0:T(8,128)(2,1)} %k_ref.3) | copy-start | bytes 786436
  1.6 0.9 %copy-start.3 = (bf16[1024,128]{1,0:T(8,128)(2,1)S(1)}, bf16[1024,128]{1,0:T(8,128)(2,1)}, u32[]{:S(2)}) copy-start(bf16[1024,128]{1,0:T(8,128)(2,1)} %v_ref.3) | copy-start | bytes 786436
  2.5 0.7 copy-start.5
  3.2 24.1 %copy-start.7 = (s32[8,6]{1,0:T(8,128)S(1)}, s32[8,6]{1,0:T(8,128)}, u32[]{:S(2)}) copy-start(s32[8,6]{1,0:T(8,128)} %param.10) | copy-start | bytes 580
  3.2 34.4 %copy-start = (bf16[1024,1024]{1,0:T(8,128)(2,1)S(1)}, bf16[1024,1024]{1,0:T(8,128)(2,1)}, u32[]{:S(2)}) copy-start(bf16[1024,1024]{1,0:T(8,128)(2,1)} %q_ref.1) | copy-start | bytes 6291460
  3.2 34.4 %copy-start.2 = (bf16[1024,128]{1,0:T(8,128)(2,1)S(1)}, bf16[1024,128]{1,0:T(8,128)(2,1)}, u32[]{:S(2)}) copy-start(bf16[1024,128]{1,0:T(8,128)(2,1)} %k_ref.3) | copy-start | bytes 786436
  3.2 34.4 %copy-start.4 = (bf16[1024,128]{1,0:T(8,128)(2,1)S(1)}, bf16[1024,128]{1,0:T(8,128)(2,1)}, u32[]{:S(2)}) copy-start(bf16[1024,128]{1,0:T(8,128)(2,1)} %v_ref.3) | copy-start | bytes 786436
  3.2 34.4 %copy-start.6 = (s32[8]{0:T(128)S(1)}, s32[8]{0:T(128)}, u32[]{:S(2)}) copy-start(s32[8]{0:T(128)} %count_ref.5) | copy-start | bytes 100
  23.4 14.2 %all-to-all-start.1 = ((bf16[32,48,128]{2,1,0:T(8,128)(2,1)}), bf16[32,48,128]{2,1,0:T(8,128)(2,1)S(1)}, u32[]{:S(2)}, u32[]{:S(2)}) async-start(bf16[32,48,128]{2,1,0:T(8,128)(2,1)} %stack.1), calls=%async_computation.1 | async-start | bytes 786432 | tf_op jit(solution)/shard_map/all_to_all | solution.py:324

commit v3 on v2

--- a/solution.py
+++ b/solution.py
@@ -21,6 +21,8 @@
 SCALE = HD ** (-0.5)
 LOG2E = 1.4426950408889634
 MIB = 1024 * 1024
+VMEM_A = 50 * MIB
+VMEM_Q = 40 * MIB
 
 F32 = jnp.float32
 BF16 = jnp.bfloat16
@@ -55,7 +57,6 @@
             pl.BlockSpec(memory_space=pltpu.VMEM),
         ],
         out_specs=pl.BlockSpec(memory_space=pltpu.VMEM),
-        compiler_params=pltpu.CompilerParams(vmem_limit_bytes=8 * MIB),
         name="pack",
     )(count, keys, values)
 
@@ -135,6 +136,12 @@
     return lax.dot_general(a, b, (((0,), (0,)), ((), ())), preferred_element_type=F32)
 
 
+def table_place(ids_ref, base, b, j):
+    ident = ids_ref[b, j]
+    place = jnp.where(ident >= base, ident - base, OWN + j)
+    return pl.multiple_of(place * BLK, BLK)
+
+
 def attn_kernel(
     ids_ref,
     count_ref,
@@ -144,11 +151,11 @@
     k_ref,
     v_ref,
     ext_ref,
-    dq_ref,
+    ds_ref,
+    kt,
     dk_ref,
     dv_ref,
     back_ref,
-    kt,
     vt,
     dke,
     dve,
@@ -181,9 +188,7 @@
     causal = key_pos <= row_pos
 
     def table_row(j):
-        ident = ids_ref[b * MAXA + j]
-        place = jnp.where(ident >= base, ident - base, OWN + j)
-        return pl.multiple_of(place * BLK, BLK)
+        return table_place(ids_ref, base, b, j)
 
     def rows_of(ref, c):
         return jnp.concatenate(
@@ -226,6 +231,7 @@
             ds = p * (d_scr[pl.ds(j * BLK, BLK), :] - delta)
             ps.append(p.astype(BF16))
             dss.append(ds.astype(BF16))
+            ds_ref[0, pl.ds(j * BLK, BLK), c * CHUNK : (c + 1) * CHUNK] = dss[-1]
         p_all = jnp.concatenate(ps, axis=0)
         ds_all = jnp.concatenate(dss, axis=0)
         dv = nn(p_all, rows_of(o_ref, c))
@@ -236,10 +242,6 @@
         else:
             dva[pl.ds(0, nk), :] += dv
             dka[pl.ds(0, nk), :] += dk
-        g = tn(kb[pl.ds(0, nk), :], ds_all) * SCALE
-        for h in range(heads):
-            at = c * CHUNK + h * HD
-            dq_ref[:, at : at + HD] = g[:, h * HD : (h + 1) * HD].T.astype(BF16)
 
     for n in range(MAXA + 1):
 
@@ -284,13 +286,13 @@
                 whole((SHARDS, PIECE, HD)),
             ],
             out_specs=[
-                pl.BlockSpec((BLK, ROWS), lambda b, *_: (b, 0)),
+                pl.BlockSpec((1, (MAXA + 1) * BLK, ROWS), lambda b, *_: (b, 0, 0)),
+                whole((tiles * BLK, HD)),
                 whole((OWN * BLK, HD)),
                 whole((OWN * BLK, HD)),
                 whole((SHARDS, PIECE, HD)),
             ],
             scratch_shapes=[
-                pltpu.VMEM((tiles * BLK, HD), BF16),
                 pltpu.VMEM((tiles * BLK, HD), BF16),
                 pltpu.VMEM((tiles * BLK, HD), F32),
                 pltpu.VMEM((tiles * BLK, HD), F32),
@@ -307,14 +309,55 @@
             * 2,
         ),
         out_shape=(
-            jax.ShapeDtypeStruct((OWN * BLK, ROWS), BF16),
+            jax.ShapeDtypeStruct((OWN, (MAXA + 1) * BLK, ROWS), BF16),
+            jax.ShapeDtypeStruct((tiles * BLK, HD), BF16),
             jax.ShapeDtypeStruct((OWN * BLK, HD), F32),
             jax.ShapeDtypeStruct((OWN * BLK, HD), F32),
             jax.ShapeDtypeStruct((SHARDS, PIECE, HD), BF16),
         ),
-        compiler_params=pltpu.CompilerParams(vmem_limit_bytes=48 * MIB),
+        compiler_params=pltpu.CompilerParams(vmem_limit_bytes=VMEM_A),
         name="attention",
     )(ids, count, base, queries, grad_out, keys, values, ext)
+
+
+def query_kernel(ids_ref, count_ref, base_ref, ds_ref, kt_ref, dq_ref, kb):
+    b = pl.program_id(0)
+    count = count_ref[b]
+    for n in range(MAXA + 1):
+
+        @pl.when(count == n)
+        def _(n=n):
+            places = [table_place(ids_ref, base_ref[0], b, j) for j in range(n)]
+            places.append(pl.multiple_of(b * BLK, BLK))
+            for j in range(n + 1):
+                kb[pl.ds(j * BLK, BLK), :] = kt_ref[pl.ds(places[j], BLK), :]
+            nk = (n + 1) * BLK
+            g = tn(kb[pl.ds(0, nk), :], ds_ref[0, pl.ds(0, nk), :]) * SCALE
+            for h in range(HQ):
+                head = slice(h * HD, (h + 1) * HD)
+                dq_ref[:, head] = g[:, head].T.astype(BF16)
+
+
+def query_grads(ids, count, base, dscores, table):
+    return pl.pallas_call(
+        query_kernel,
+        grid_spec=pltpu.PrefetchScalarGridSpec(
+            num_scalar_prefetch=3,
+            grid=(OWN,),
+            in_specs=[
+                pl.BlockSpec((1, (MAXA + 1) * BLK, ROWS), lambda b, *_: (b, 0, 0)),
+                pl.BlockSpec(table.shape, lambda b, *_: (0, 0)),
+            ],
+            out_specs=pl.BlockSpec((BLK, ROWS), lambda b, *_: (b, 0)),
+            scratch_shapes=[pltpu.VMEM(((MAXA + 1) * BLK, HD), BF16)],
+        ),
+        out_shape=jax.ShapeDtypeStruct((OWN * BLK, ROWS), BF16),
+        compiler_params=pltpu.CompilerParams(vmem_limit_bytes=VMEM_Q),
+        cost_estimate=pl.CostEstimate(
+            flops=int(1e10), bytes_accessed=16 * MIB, transcendentals=0
+        ),
+        name="query_grads",
+    )(ids, count, base, dscores, table)
 
 
 def body(queries, keys, values, grad_out, ancestor_ids, ancestor_count):
@@ -322,9 +365,9 @@
     mine = pack(keys, values, ancestor_count)
     pieces = lax.all_to_all(mine, "ctx", 0, 0, tiled=True)
     ext = lax.all_to_all(stack(pieces), "ctx", 0, 0, tiled=True)
-    grad_queries, dk, dv, back = attention(
-        ancestor_ids.reshape(-1), ancestor_count, base, queries, grad_out, keys, values, ext
-    )
+    scalars = (ancestor_ids, ancestor_count, base)
+    dscores, table, dk, dv, back = attention(*scalars, queries, grad_out, keys, values, ext)
+    grad_queries = query_grads(*scalars, dscores, table)
     sums = segsum(pieces, lax.all_to_all(back, "ctx", 0, 0, tiled=True))
     terms = lax.all_to_all(sums, "ctx", 0, 0, tiled=True)
     grad_keys, grad_values = final(ancestor_count, dk, dv, terms)

time: 91.5 us -> 91.7 us (level); the launches traced: 92.4 us -> 90.6 us
  blocking collectives: 53.9 us -> 41 us
  Pallas kernels: 21 us -> 30.8 us
  starting transfers between devices: 3.9 us -> 7.8 us
  local copies, waits for them, and re-layouts: 2.65 us -> 0.02 us
    all_to_all x1 -> x0, blocking collectives: 13.8 us -> none  [body(): terms = lax.all_to_all(sums, 'ctx', 0, 0, tiled=True)]
    pallas_call x0 -> x1, Pallas kernels: none -> 10.4 us  [query_grads(): pl.pallas_call(query_kernel, grid_spec=pltpu.PrefetchScalarGridSpec(num_s...]
    all_to_all x0 -> x1, starting transfers between devices: none -> 3.9 us  [body(): terms = lax.all_to_all(sums, 'ctx', 0, 0, tiled=True)]
    pallas_call x1, Pallas kernels: 17.9 us -> 15.2 us  [attention(): pl.pallas_call(attn_kernel, grid_spec=pltpu.PrefetchScalarGridSpec(num_sc...]
    unnamed x16 -> x8, local copies, waits for them, and re-layouts: 2.57 us -> 0.02 us
    pallas_call x1, Pallas kernels: 0.63 us -> 1.93 us  [pack(): pl.pallas_call(pack_kernel, out_shape=jax.ShapeDtypeStruct((SHARDS, PIECE...]
  transfers between devices with their start and end apart: 1 -> 2, of which waited for: 1 -> 1; matrix products, arithmetic and copies ran while one was open for 0% -> 0% of each run, Pallas kernels for 0% -> 12%
where the time goes in v3:
time: 91.7 us; the launch traced here: 90.6 us
  blocking collectives  41 us (45%)
  Pallas kernels  30.8 us (34%)
  waiting for transfers between devices  10.3 us (11%)
  starting transfers between devices  7.8 us (9%)
    all_to_all x1, blocking collectives, body(): sums = segsum(pieces, lax.all_to_all(back, 'ctx', 0, 0, tiled=True))  22.2 us
    all_to_all x1, blocking collectives, body(): pieces = lax.all_to_all(mine, 'ctx', 0, 0, tiled=True)  18.8 us
    pallas_call x1, Pallas kernels, attention(): pl.pallas_call(attn_kernel, grid_spec=pltpu.PrefetchScalarGridSpec(num_sc...  15.2 us
    pallas_call x1, Pallas kernels, query_grads(): pl.pallas_call(query_kernel, grid_spec=pltpu.PrefetchScalarGridSpec(num_s...  10.4 us
    all_to_all x1, waiting for transfers between devices, body(): ext = lax.all_to_all(stack(pieces), 'ctx', 0, 0, tiled=True)  10.3 us
    all_to_all x1, starting transfers between devices, body(): ext = lax.all_to_all(stack(pieces), 'ctx', 0, 0, tiled=True)  3.9 us
    all_to_all x1, starting transfers between devices, body(): terms = lax.all_to_all(sums, 'ctx', 0, 0, tiled=True)  3.9 us
    pallas_call x1, Pallas kernels, pack(): pl.pallas_call(pack_kernel, out_shape=jax.ShapeDtypeStruct((SHARDS, PIECE...  1.93 us
  transfers between devices with their start and end apart: 2, of which 1 were waited for; matrix products, arithmetic and copies ran while one was open for 0% of the time, Pallas kernels for 12%

profile of v3, /device:TPU:1, one launch (start us, length us, event | category | flops | bytes accessed | tf_op | source)
XLA Modules:
  0.0 90.6 jit_solution(10644621930910096443)
XLA Ops:
  0.6 0.0 copy-start.2
  0.6 0.0 copy-start
  0.7 0.0 copy-start.1
  0.7 0.0 copy-start.3
  0.7 1.9 %pack.1 = bf16[32,48,128]{2,1,0:T(8,128)(2,1)} custom-call(s32[8]{0:T(128)} %count_ref.7, bf16[1024,128]{1,0:T(8,128)(2,1)} %k_ref.3, bf16[1024,128]{1,0:T(8,128)(2,1)} %v_ref.3), custom_call_target="tpu_custom_call" | custom-call | tf_op jit(solution)/shard_map/pack/pallas_call | solution.py:51
  2.6 18.8 %all_to_all.20.in_ref.flag_ref = bf16[32,48,128]{2,1,0:T(8,128)(2,1)S(1)} all-to-all(bf16[32,48,128]{2,1,0:T(8,128)(2,1)} %pack.1), channel_id=1, replica_groups=mesh['ctx'=32,'head'=4,'rep'=1] {'ctx'}, dimensions={0} | all-to-all | bytes 786432 | tf_op jit(solution)/shard_map/all_to_all | solution.py:366
  21.4 0.8 stack.1
  22.2 3.9 %all-to-all-start.1 = ((bf16[32,48,128]{2,1,0:T(8,128)(2,1)}), bf16[32,48,128]{2,1,0:T(8,128)(2,1)S(1)}, u32[]{:S(2)}, u32[]{:S(2)}) async-start(bf16[32,48,128]{2,1,0:T(8,128)(2,1)} %stack.1), calls=%async_computation.1 | async-start | bytes 786432 | tf_op jit(solution)/shard_map/all_to_all | solution.py:367
  26.1 10.3 %all-to-all-done.1.ext_ref = bf16[32,48,128]{2,1,0:T(8,128)(2,1)S(1)} async-done(((bf16[32,48,128]{2,1,0:T(8,128)(2,1)}), bf16[32,48,128]{2,1,0:T(8,128)(2,1)S(1)}, u32[]{:S(2)}, u32[]{:S(2)}) %all-to-all-start.1) | async-done | bytes 393248 | tf_op jit(solution)/shard_map/all_to_all | solution.py:367
  36.4 0.0 copy-done.2
  36.4 0.0 copy-done
  36.4 0.0 copy-done.1
  36.4 0.0 copy-done.3
  36.4 15.2 %attention.1 = (bf16[8,896,1024]{2,1,0:T(8,128)(2,1)}, bf16[1792,128]{1,0:T(8,128)(2,1)S(1)}, f32[1024,128]{1,0:T(8,128)S(1)}, f32[1024,128]{1,0:T(8,128)S(1)}, bf16[32,48,128]{2,1,0:T(8,128)(2,1)S(1)}) custom-call(s32[8,6]{1,0:T(8,128)S(1)} %copy-done.3, s32[8]{0:T(128)S(1)} %copy-done.2, s32[1]{0:T(128)} %bitcast.base_ref, bf16[1024,1024]{1,0:T(8,128)(2,1)} %q_ref.1, ...), custom_call_target="tpu_custom_call" | custom-call | tf_op jit(solution)/shard_map/attention/pallas_call | solution.py:276
  51.6 22.2 %all_to_all.21.in_ref = bf16[32,48,128]{2,1,0:T(8,128)(2,1)S(1)} all-to-all(bf16[32,48,128]{2,1,0:T(8,128)(2,1)S(1)} %get-tuple-element.14), channel_id=1, replica_groups=mesh['ctx'=32,'head'=4,'rep'=1] {'ctx'}, dimensions={0} | all-to-all | bytes 786432 | tf_op jit(solution)/shard_map/all_to_all | solution.py:371
  73.8 0.9 %segsum.1 = bf16[32,48,128]{2,1,0:T(8,128)(2,1)} custom-call(bf16[32,48,128]{2,1,0:T(8,128)(2,1)S(1)} %all_to_all.20.in_ref.flag_ref, bf16[32,48,128]{2,1,0:T(8,128)(2,1)S(1)} %all_to_all.21.in_ref), custom_call_target="tpu_custom_call" | custom-call | tf_op jit(solution)/shard_map/segsum/pallas_call | solution.py:92
  74.7 3.9 %all-to-all-start.3 = ((bf16[32,48,128]{2,1,0:T(8,128)(2,1)}), bf16[32,48,128]{2,1,0:T(8,128)(2,1)S(1)}, u32[]{:S(2)}, u32[]{:S(2)}) async-start(bf16[32,48,128]{2,1,0:T(8,128)(2,1)} %segsum.1), calls=%async_computation.3 | async-start | bytes 786432 | tf_op jit(solution)/shard_map/all_to_all | solution.py:372
  78.7 10.4 %query_grads.1 = bf16[1024,1024]{1,0:T(8,128)(2,1)} custom-call(s32[8,6]{1,0:T(8,128)S(1)} %copy-done.3, s32[8]{0:T(128)S(1)} %copy-done.2, s32[1]{0:T(128)} %bitcast.base_ref, bf16[8,896,1024]{2,1,0:T(8,128)(2,1)} %get-tuple-element.10.ds_ref, bf16[1792,128]{1,0:T(8,128)(2,1)S(1)} %get-tuple-element.11.kt_ref), custom_call_target="tpu_custom_call" | custom-call | flops 10000000000 | bytes 16777216 | tf_op jit(solution)/shard_map/query_grads/pallas_call | solution.py:342
  89.1 0.0 all-to-all-done.3.in_ref
  89.1 1.5 %final.1 = (bf16[1024,128]{1,0:T(8,128)(2,1)}, bf16[1024,128]{1,0:T(8,128)(2,1)}) custom-call(s32[8]{0:T(128)S(1)} %copy-done.2, f32[1024,128]{1,0:T(8,128)S(1)} %get-tuple-element.12.dk_ref, f32[1024,128]{1,0:T(8,128)S(1)} %get-tuple-element.13.dv_ref, bf16[32,48,128]{2,1,0:T(8,128)(2,1)S(1)} %all-to-all-done.3.in_ref), custom_call_target="tpu_custom_call" | custom-call | tf_op jit(solution)/shard_map/final/pallas_call | solution.py:116
Async XLA Ops:
  0.6 35.8 %copy-start.2 = (s32[8]{0:T(128)S(1)}, s32[8]{0:T(128)}, u32[]{:S(2)}) copy-start(s32[8]{0:T(128)} %count_ref.7) | copy-start | bytes 100
  0.6 35.8 %copy-start = (bf16[1024,128]{1,0:T(8,128)(2,1)S(1)}, bf16[1024,128]{1,0:T(8,128)(2,1)}, u32[]{:S(2)}) copy-start(bf16[1024,128]{1,0:T(8,128)(2,1)} %k_ref.3) | copy-start | bytes 786436
  0.7 35.7 %copy-start.1 = (bf16[1024,128]{1,0:T(8,128)(2,1)S(1)}, bf16[1024,128]{1,0:T(8,128)(2,1)}, u32[]{:S(2)}) copy-start(bf16[1024,128]{1,0:T(8,128)(2,1)} %v_ref.3) | copy-start | bytes 786436
  0.7 35.7 %copy-start.3 = (s32[8,6]{1,0:T(8,128)S(1)}, s32[8,6]{1,0:T(8,128)}, u32[]{:S(2)}) copy-start(s32[8,6]{1,0:T(8,128)} %ids_ref.3) | copy-start | bytes 580
  22.2 14.2 %all-to-all-start.1 = ((bf16[32,48,128]{2,1,0:T(8,128)(2,1)}), bf16[32,48,128]{2,1,0:T(8,128)(2,1)S(1)}, u32[]{:S(2)}, u32[]{:S(2)}) async-start(bf16[32,48,128]{2,1,0:T(8,128)(2,1)} %stack.1), calls=%async_computation.1 | async-start | bytes 786432 | tf_op jit(solution)/shard_map/all_to_all | solution.py:367
  74.7 14.3 %all-to-all-start.3 = ((bf16[32,48,128]{2,1,0:T(8,128)(2,1)}), bf16[32,48,128]{2,1,0:T(8,128)(2,1)S(1)}, u32[]{:S(2)}, u32[]{:S(2)}) async-start(bf16[32,48,128]{2,1,0:T(8,128)(2,1)} %segsum.1), calls=%async_computation.3 | async-start | bytes 786432 | tf_op jit(solution)/shard_map/all_to_all | solution.py:372

commit v4 on v3

--- a/solution.py
+++ b/solution.py
@@ -14,7 +14,7 @@
 OWN = 8
 SHARDS = 32
 ROWS = HQ * BLK
-CHUNK = 256
+CHUNK = 512
 PIECE = 8 * MAXA
 MARK = 1e30
 MARK_MIN = 1e29
@@ -145,7 +145,6 @@
 def attn_kernel(
     ids_ref,
     count_ref,
-    base_ref,
     q_ref,
     o_ref,
     k_ref,
@@ -166,7 +165,7 @@
     *slots,
 ):
     b = pl.program_id(0)
-    base = base_ref[0]
+    base = lax.axis_index("ctx") * OWN
 
     @pl.when(b == 0)
     def _():
@@ -195,47 +194,46 @@
             [ref[:, c * CHUNK + h * HD : c * CHUNK + (h + 1) * HD] for h in range(heads)], axis=0
         )
 
-    def first(n, c):
-        e_scr, d_scr, g_scr = slots[3 * (c % 2) : 3 * (c % 2) + 3]
+    def slot(c):
+        return slots[3 * (c % 2) : 3 * (c % 2) + 3]
+
+    def scores(n, c):
         nk = (n + 1) * BLK
-        s_all = nt(kb[pl.ds(0, nk), :], rows_of(q_ref, c))
-        d_all = nt(vb[pl.ds(0, nk), :], rows_of(o_ref, c))
-        tops, sums, dots = [], [], []
-        for j in range(n + 1):
-            s = s_all[j * BLK : (j + 1) * BLK]
-            d = d_all[j * BLK : (j + 1) * BLK]
-            if j == n:
-                s = jnp.where(causal, s, -jnp.inf)
-            top = jnp.max(s, axis=0, keepdims=True)
-            e = jnp.exp2((s - top) * coef)
-            tops.append(top)
-            sums.append(jnp.sum(e, axis=0, keepdims=True))
-            dots.append(jnp.sum(e * d, axis=0, keepdims=True))
-            e_scr[pl.ds(j * BLK, BLK), :] = e
-            d_scr[pl.ds(j * BLK, BLK), :] = d
-        top = functools.reduce(jnp.maximum, tops)
-        factors = [jnp.exp2((t - top) * coef) for t in tops]
-        inv = 1.0 / sum(f * x for f, x in zip(factors, sums))
-        delta = sum(f * x for f, x in zip(factors, dots)) * inv
-        for j in range(n + 1):
-            g_scr[j : j + 1, :] = factors[j] * inv
+        return nt(kb[pl.ds(0, nk), :], rows_of(q_ref, c)), nt(vb[pl.ds(0, nk), :], rows_of(o_ref, c))
+
+    def keep(n, c, j, both):
+        e_scr, d_scr, _ = slot(c)
+        s, d = (x[j * BLK : (j + 1) * BLK] for x in both)
+        if j == n:
+            s = jnp.where(causal, s, -jnp.inf)
+        top = jnp.max(s, axis=0, keepdims=True)
+        e = jnp.exp2((s - top) * coef)
+        e_scr[pl.ds(j * BLK, BLK), :] = e
+        d_scr[pl.ds(j * BLK, BLK), :] = d
+        return top, jnp.sum(e, axis=0, keepdims=True), jnp.sum(e * d, axis=0, keepdims=True)
+
+    def merge(c, stats):
+        g_scr = slot(c)[2]
+        top = functools.reduce(jnp.maximum, [t for t, _, _ in stats])
+        factors = [jnp.exp2((t - top) * coef) for t, _, _ in stats]
+        inv = 1.0 / sum(f * x for f, (_, x, _) in zip(factors, stats))
+        delta = sum(f * x for f, (_, _, x) in zip(factors, stats)) * inv
+        for j, f in enumerate(factors):
+            g_scr[j : j + 1, :] = f * inv
         g_scr[MAXA + 1 : MAXA + 2, :] = delta
 
-    def second(n, c):
-        e_scr, d_scr, g_scr = slots[3 * (c % 2) : 3 * (c % 2) + 3]
+    def weigh(c, j):
+        e_scr, d_scr, g_scr = slot(c)
+        p = e_scr[pl.ds(j * BLK, BLK), :] * g_scr[j : j + 1, :]
+        ds = p * (d_scr[pl.ds(j * BLK, BLK), :] - g_scr[MAXA + 1 : MAXA + 2, :])
+        ds = ds.astype(BF16)
+        ds_ref[0, pl.ds(j * BLK, BLK), c * CHUNK : (c + 1) * CHUNK] = ds
+        return p.astype(BF16), ds
+
+    def add(n, c, tiles):
         nk = (n + 1) * BLK
-        delta = g_scr[MAXA + 1 : MAXA + 2, :]
-        ps, dss = [], []
-        for j in range(n + 1):
-            p = e_scr[pl.ds(j * BLK, BLK), :] * g_scr[j : j + 1, :]
-            ds = p * (d_scr[pl.ds(j * BLK, BLK), :] - delta)
-            ps.append(p.astype(BF16))
-            dss.append(ds.astype(BF16))
-            ds_ref[0, pl.ds(j * BLK, BLK), c * CHUNK : (c + 1) * CHUNK] = dss[-1]
-        p_all = jnp.concatenate(ps, axis=0)
-        ds_all = jnp.concatenate(dss, axis=0)
-        dv = nn(p_all, rows_of(o_ref, c))
-        dk = nn(ds_all, rows_of(q_ref, c))
+        dv = nn(jnp.concatenate([p for p, _ in tiles], axis=0), rows_of(o_ref, c))
+        dk = nn(jnp.concatenate([ds for _, ds in tiles], axis=0), rows_of(q_ref, c))
         if c == 0:
             dva[pl.ds(0, nk), :] = dv
             dka[pl.ds(0, nk), :] = dk
@@ -252,11 +250,20 @@
                 kb[pl.ds(j * BLK, BLK), :] = kt[pl.ds(places[j], BLK), :]
                 vb[pl.ds(j * BLK, BLK), :] = vt[pl.ds(places[j], BLK), :]
             chunks = ROWS // CHUNK
-            first(n, 0)
+            both = scores(n, 0)
+            merge(0, [keep(n, 0, j, both) for j in range(n + 1)])
             for c in range(chunks):
-                if c + 1 < chunks:
-                    first(n, c + 1)
-                second(n, c)
+                more = c + 1 < chunks
+                if more:
+                    both = scores(n, c + 1)
+                tiles, stats = [], []
+                for j in range(n + 1):
+                    tiles.append(weigh(c, j))
+                    if more:
+                        stats.append(keep(n, c + 1, j, both))
+                add(n, c, tiles)
+                if more:
+                    merge(c + 1, stats)
             for j in range(n + 1):
                 dke[pl.ds(places[j], BLK), :] += dka[pl.ds(j * BLK, BLK), :]
                 dve[pl.ds(places[j], BLK), :] += dva[pl.ds(j * BLK, BLK), :]
@@ -270,13 +277,13 @@
             back_ref[pl.ds(half * 16, 16)] = jnp.concatenate(parts, axis=1).astype(BF16)
 
 
-def attention(ids, count, base, queries, grad_out, keys, values, ext):
+def attention(ids, count, queries, grad_out, keys, values, ext):
     whole = lambda shape: pl.BlockSpec(shape, lambda b, *_: (0,) * len(shape))
     tiles = OWN + MAXA
     return pl.pallas_call(
         attn_kernel,
         grid_spec=pltpu.PrefetchScalarGridSpec(
-            num_scalar_prefetch=3,
+            num_scalar_prefetch=2,
             grid=(OWN,),
             in_specs=[
                 pl.BlockSpec((BLK, ROWS), lambda b, *_: (b, 0)),
@@ -317,17 +324,18 @@
         ),
         compiler_params=pltpu.CompilerParams(vmem_limit_bytes=VMEM_A),
         name="attention",
-    )(ids, count, base, queries, grad_out, keys, values, ext)
-
-
-def query_kernel(ids_ref, count_ref, base_ref, ds_ref, kt_ref, dq_ref, kb):
+    )(ids, count, queries, grad_out, keys, values, ext)
+
+
+def query_kernel(ids_ref, count_ref, ds_ref, kt_ref, dq_ref, kb):
     b = pl.program_id(0)
+    base = lax.axis_index("ctx") * OWN
     count = count_ref[b]
     for n in range(MAXA + 1):
 
         @pl.when(count == n)
         def _(n=n):
-            places = [table_place(ids_ref, base_ref[0], b, j) for j in range(n)]
+            places = [table_place(ids_ref, base, b, j) for j in range(n)]
             places.append(pl.multiple_of(b * BLK, BLK))
             for j in range(n + 1):
                 kb[pl.ds(j * BLK, BLK), :] = kt_ref[pl.ds(places[j], BLK), :]
@@ -338,11 +346,11 @@
                 dq_ref[:, head] = g[:, head].T.astype(BF16)
 
 
-def query_grads(ids, count, base, dscores, table):
+def query_grads(ids, count, dscores, table):
     return pl.pallas_call(
         query_kernel,
         grid_spec=pltpu.PrefetchScalarGridSpec(
-            num_scalar_prefetch=3,
+            num_scalar_prefetch=2,
             grid=(OWN,),
             in_specs=[
                 pl.BlockSpec((1, (MAXA + 1) * BLK, ROWS), lambda b, *_: (b, 0, 0)),
@@ -357,15 +365,14 @@
             flops=int(1e10), bytes_accessed=16 * MIB, transcendentals=0
         ),
         name="query_grads",
-    )(ids, count, base, dscores, table)
+    )(ids, count, dscores, table)
 
 
 def body(queries, keys, values, grad_out, ancestor_ids, ancestor_count):
-    base = (lax.axis_index("ctx") * OWN).astype(jnp.int32).reshape(1)
     mine = pack(keys, values, ancestor_count)
     pieces = lax.all_to_all(mine, "ctx", 0, 0, tiled=True)
     ext = lax.all_to_all(stack(pieces), "ctx", 0, 0, tiled=True)
-    scalars = (ancestor_ids, ancestor_count, base)
+    scalars = (ancestor_ids, ancestor_count)
     dscores, table, dk, dv, back = attention(*scalars, queries, grad_out, keys, values, ext)
     grad_queries = query_grads(*scalars, dscores, table)
     sums = segsum(pieces, lax.all_to_all(back, "ctx", 0, 0, tiled=True))

time: 91.7 us -> 89 us (0.971)
  blocking collectives: 41 us -> 51.3 us
  waiting for transfers between devices: 10.3 us -> 0.01 us
  starting transfers between devices: 7.8 us -> 4.08 us
  Pallas kernels: 30.8 us -> 32 us
    all_to_all x0 -> x1, blocking collectives: none -> 13.8 us  [body(): ext = lax.all_to_all(stack(pieces), 'ctx', 0, 0, tiled=True)]
    all_to_all x1 -> x0, waiting for transfers between devices: 10.3 us -> none  [body(): ext = lax.all_to_all(stack(pieces), 'ctx', 0, 0, tiled=True)]
    all_to_all x1 -> x0, starting transfers between devices: 3.9 us -> none  [body(): ext = lax.all_to_all(stack(pieces), 'ctx', 0, 0, tiled=True)]
    all_to_all x1, blocking collectives: 22.2 us -> 18.7 us  [body(): sums = segsum(pieces, lax.all_to_all(back, 'ctx', 0, 0, tiled=True))]
    pallas_call x1, Pallas kernels: 15.2 us -> 17 us  [attention(): pl.pallas_call(attn_kernel, grid_spec=pltpu.PrefetchScalarGridSpec(num_sc...]
  transfers between devices with their start and end apart: 2 -> 1, of which waited for: 1 -> 0; matrix products, arithmetic and copies ran while one was open for 0% -> 0% of each run, Pallas kernels for 12% -> 12%
where the time goes in v4:
time: 89 us; the launch traced here: 88.1 us
  blocking collectives  51.3 us (58%)
  Pallas kernels  32 us (36%)
  starting transfers between devices  4.08 us (5%)
    all_to_all x1, blocking collectives, body(): pieces = lax.all_to_all(mine, 'ctx', 0, 0, tiled=True)  18.8 us
    all_to_all x1, blocking collectives, body(): sums = segsum(pieces, lax.all_to_all(back, 'ctx', 0, 0, tiled=True))  18.7 us
    pallas_call x1, Pallas kernels, attention(): pl.pallas_call(attn_kernel, grid_spec=pltpu.PrefetchScalarGridSpec(num_sc...  17 us
    all_to_all x1, blocking collectives, body(): ext = lax.all_to_all(stack(pieces), 'ctx', 0, 0, tiled=True)  13.8 us
    pallas_call x1, Pallas kernels, query_grads(): pl.pallas_call(query_kernel, grid_spec=pltpu.PrefetchScalarGridSpec(num_s...  10.5 us
    all_to_all x1, starting transfers between devices, body(): terms = lax.all_to_all(sums, 'ctx', 0, 0, tiled=True)  4.08 us
    pallas_call x1, Pallas kernels, pack(): pl.pallas_call(pack_kernel, out_shape=jax.ShapeDtypeStruct((SHARDS, PIECE...  1.93 us
  transfers between devices with their start and end apart: 1, of which 0 were waited for; matrix products, arithmetic and copies ran while one was open for 0% of the time, Pallas kernels for 12%

profile of v4, /device:TPU:1, one launch (start us, length us, event | category | flops | bytes accessed | tf_op | source)
XLA Modules:
  0.0 88.1 jit_solution(18361113484107365953)
XLA Ops:
  0.6 0.0 copy-start.2
  0.6 0.0 copy-start
  0.7 0.0 copy-start.1
  0.7 0.0 copy-start.3
  0.7 1.9 %pack.1 = bf16[32,48,128]{2,1,0:T(8,128)(2,1)} custom-call(s32[8]{0:T(128)} %count_ref.7, bf16[1024,128]{1,0:T(8,128)(2,1)} %k_ref.3, bf16[1024,128]{1,0:T(8,128)(2,1)} %v_ref.3), custom_call_target="tpu_custom_call" | custom-call | tf_op jit(solution)/shard_map/pack/pallas_call | solution.py:51
  2.6 18.8 %all_to_all.20.in_ref.flag_ref = bf16[32,48,128]{2,1,0:T(8,128)(2,1)S(1)} all-to-all(bf16[32,48,128]{2,1,0:T(8,128)(2,1)} %pack.1), channel_id=1, replica_groups=mesh['ctx'=32,'head'=4,'rep'=1] {'ctx'}, dimensions={0} | all-to-all | bytes 786432 | tf_op jit(solution)/shard_map/all_to_all | solution.py:373
  21.4 0.1 stack.1
  21.5 13.8 %all_to_all.21.ext_ref = bf16[32,48,128]{2,1,0:T(8,128)(2,1)S(1)} all-to-all(bf16[32,48,128]{2,1,0:T(8,128)(2,1)S(1)} %stack.1), channel_id=1, replica_groups=mesh['ctx'=32,'head'=4,'rep'=1] {'ctx'}, dimensions={0} | all-to-all | bytes 786432 | tf_op jit(solution)/shard_map/all_to_all | solution.py:374
  35.2 0.0 copy-done.2
  35.2 0.0 copy-done
  35.2 0.0 copy-done.1
  35.2 0.0 copy-done.3
  35.2 17.0 %attention.1 = (bf16[8,896,1024]{2,1,0:T(8,128)(2,1)}, bf16[1792,128]{1,0:T(8,128)(2,1)S(1)}, f32[1024,128]{1,0:T(8,128)S(1)}, f32[1024,128]{1,0:T(8,128)S(1)}, bf16[32,48,128]{2,1,0:T(8,128)(2,1)S(1)}) custom-call(s32[8,6]{1,0:T(8,128)S(1)} %copy-done.3, s32[8]{0:T(128)S(1)} %copy-done.2, bf16[1024,1024]{1,0:T(8,128)(2,1)} %q_ref.1, ...), custom_call_target="tpu_custom_call" | custom-call | tf_op jit(solution)/shard_map/attention/pallas_call | solution.py:283
  52.3 18.7 %all_to_all.22.in_ref = bf16[32,48,128]{2,1,0:T(8,128)(2,1)S(1)} all-to-all(bf16[32,48,128]{2,1,0:T(8,128)(2,1)S(1)} %get-tuple-element.14), channel_id=1, replica_groups=mesh['ctx'=32,'head'=4,'rep'=1] {'ctx'}, dimensions={0} | all-to-all | bytes 786432 | tf_op jit(solution)/shard_map/all_to_all | solution.py:378
  71.0 0.9 %segsum.1 = bf16[32,48,128]{2,1,0:T(8,128)(2,1)} custom-call(bf16[32,48,128]{2,1,0:T(8,128)(2,1)S(1)} %all_to_all.20.in_ref.flag_ref, bf16[32,48,128]{2,1,0:T(8,128)(2,1)S(1)} %all_to_all.22.in_ref), custom_call_target="tpu_custom_call" | custom-call | tf_op jit(solution)/shard_map/segsum/pallas_call | solution.py:92
  71.9 4.1 %all-to-all-start.3 = ((bf16[32,48,128]{2,1,0:T(8,128)(2,1)}), bf16[32,48,128]{2,1,0:T(8,128)(2,1)S(1)}, u32[]{:S(2)}, u32[]{:S(2)}) async-start(bf16[32,48,128]{2,1,0:T(8,128)(2,1)} %segsum.1), calls=%async_computation.3 | async-start | bytes 786432 | tf_op jit(solution)/shard_map/all_to_all | solution.py:379
  76.0 10.5 %query_grads.1 = bf16[1024,1024]{1,0:T(8,128)(2,1)} custom-call(s32[8,6]{1,0:T(8,128)S(1)} %copy-done.3, s32[8]{0:T(128)S(1)} %copy-done.2, bf16[8,896,1024]{2,1,0:T(8,128)(2,1)} %get-tuple-element.10.ds_ref, bf16[1792,128]{1,0:T(8,128)(2,1)S(1)} %get-tuple-element.11.kt_ref), custom_call_target="tpu_custom_call" | custom-call | flops 10000000000 | bytes 16777216 | tf_op jit(solution)/shard_map/query_grads/pallas_call | solution.py:350
  86.6 0.0 all-to-all-done.3.in_ref
  86.6 1.5 %final.1 = (bf16[1024,128]{1,0:T(8,128)(2,1)}, bf16[1024,128]{1,0:T(8,128)(2,1)}) custom-call(s32[8]{0:T(128)S(1)} %copy-done.2, f32[1024,128]{1,0:T(8,128)S(1)} %get-tuple-element.12.dk_ref, f32[1024,128]{1,0:T(8,128)S(1)} %get-tuple-element.13.dv_ref, bf16[32,48,128]{2,1,0:T(8,128)(2,1)S(1)} %all-to-all-done.3.in_ref), custom_call_target="tpu_custom_call" | custom-call | tf_op jit(solution)/shard_map/final/pallas_call | solution.py:116
Async XLA Ops:
  0.6 34.6 %copy-start.2 = (s32[8]{0:T(128)S(1)}, s32[8]{0:T(128)}, u32[]{:S(2)}) copy-start(s32[8]{0:T(128)} %count_ref.7) | copy-start | bytes 100
  0.6 34.6 %copy-start = (bf16[1024,128]{1,0:T(8,128)(2,1)S(1)}, bf16[1024,128]{1,0:T(8,128)(2,1)}, u32[]{:S(2)}) copy-start(bf16[1024,128]{1,0:T(8,128)(2,1)} %k_ref.3) | copy-start | bytes 786436
  0.7 34.6 %copy-start.1 = (bf16[1024,128]{1,0:T(8,128)(2,1)S(1)}, bf16[1024,128]{1,0:T(8,128)(2,1)}, u32[]{:S(2)}) copy-start(bf16[1024,128]{1,0:T(8,128)(2,1)} %v_ref.3) | copy-start | bytes 786436
  0.7 34.6 %copy-start.3 = (s32[8,6]{1,0:T(8,128)S(1)}, s32[8,6]{1,0:T(8,128)}, u32[]{:S(2)}) copy-start(s32[8,6]{1,0:T(8,128)} %ids_ref.3) | copy-start | bytes 580
  71.9 14.6 %all-to-all-start.3 = ((bf16[32,48,128]{2,1,0:T(8,128)(2,1)}), bf16[32,48,128]{2,1,0:T(8,128)(2,1)S(1)}, u32[]{:S(2)}, u32[]{:S(2)}) async-start(bf16[32,48,128]{2,1,0:T(8,128)(2,1)} %segsum.1), calls=%async_computation.3 | async-start | bytes 786432 | tf_op jit(solution)/shard_map/all_to_all | solution.py:379

commit v5 on v4

--- a/solution.py
+++ b/solution.py
@@ -340,10 +340,10 @@
             for j in range(n + 1):
                 kb[pl.ds(j * BLK, BLK), :] = kt_ref[pl.ds(places[j], BLK), :]
             nk = (n + 1) * BLK
-            g = tn(kb[pl.ds(0, nk), :], ds_ref[0, pl.ds(0, nk), :]) * SCALE
+            g = (tn(kb[pl.ds(0, nk), :], ds_ref[0, pl.ds(0, nk), :]) * SCALE).astype(BF16)
             for h in range(HQ):
                 head = slice(h * HD, (h + 1) * HD)
-                dq_ref[:, head] = g[:, head].T.astype(BF16)
+                dq_ref[:, head] = g[:, head].T
 
 
 def query_grads(ids, count, dscores, table):
@@ -375,7 +375,9 @@
     scalars = (ancestor_ids, ancestor_count)
     dscores, table, dk, dv, back = attention(*scalars, queries, grad_out, keys, values, ext)
     grad_queries = query_grads(*scalars, dscores, table)
-    sums = segsum(pieces, lax.all_to_all(back, "ctx", 0, 0, tiled=True))
+    got = lax.all_to_all(back, "ctx", 0, 0, tiled=True)
+    got, grad_queries = lax.optimization_barrier((got, grad_queries))
+    sums = segsum(pieces, got)
     terms = lax.all_to_all(sums, "ctx", 0, 0, tiled=True)
     grad_keys, grad_values = final(ancestor_count, dk, dv, terms)
     return (grad_queries, grad_keys, grad_values)

time: 89 us -> 91.8 us (1.031); the launches traced: 88.1 us -> 91.9 us
  starting transfers between devices: 4.08 us -> 12.1 us
  Pallas kernels: 32 us -> 29 us
  blocking collectives: 51.3 us -> 50.2 us
    all_to_all x1, starting transfers between devices: 4.08 us -> 12.1 us  [body(): got = lax.all_to_all(back, 'ctx', 0, 0, tiled=True)]
    pallas_call x1, Pallas kernels: 17 us -> 15 us  [attention(): pl.pallas_call(attn_kernel, grid_spec=pltpu.PrefetchScalarGridSpec(num_sc...]
    all_to_all x1, blocking collectives: 18.7 us -> 17.7 us  [body(): terms = lax.all_to_all(sums, 'ctx', 0, 0, tiled=True)]
  transfers between devices with their start and end apart: 1 -> 1, of which waited for: 0 -> 0; matrix products, arithmetic and copies ran while one was open for 0% -> 0% of each run, Pallas kernels for 12% -> 11%
where the time goes in v5:
time: 91.8 us; the launch traced here: 91.9 us
  blocking collectives  50.2 us (55%)
  Pallas kernels  29 us (32%)
  starting transfers between devices  12.1 us (13%)
    all_to_all x1, blocking collectives, body(): pieces = lax.all_to_all(mine, 'ctx', 0, 0, tiled=True)  18.8 us
    all_to_all x1, blocking collectives, body(): terms = lax.all_to_all(sums, 'ctx', 0, 0, tiled=True)  17.7 us
    pallas_call x1, Pallas kernels, attention(): pl.pallas_call(attn_kernel, grid_spec=pltpu.PrefetchScalarGridSpec(num_sc...  15 us
    all_to_all x1, blocking collectives, body(): ext = lax.all_to_all(stack(pieces), 'ctx', 0, 0, tiled=True)  13.8 us
    all_to_all x1, starting transfers between devices, body(): got = lax.all_to_all(back, 'ctx', 0, 0, tiled=True)  12.1 us
    pallas_call x1, Pallas kernels, query_grads(): pl.pallas_call(query_kernel, grid_spec=pltpu.PrefetchScalarGridSpec(num_s...  10.3 us
    pallas_call x1, Pallas kernels, pack(): pl.pallas_call(pack_kernel, out_shape=jax.ShapeDtypeStruct((SHARDS, PIECE...  1.93 us
  transfers between devices with their start and end apart: 1, of which 0 were waited for; matrix products, arithmetic and copies ran while one was open for 0% of the time, Pallas kernels for 11%

profile of v5, /device:TPU:1, one launch (start us, length us, event | category | flops | bytes accessed | tf_op | source)
XLA Modules:
  0.0 91.9 jit_solution(3501632580011443131)
XLA Ops:
  0.6 0.0 copy-start.2
  0.6 0.0 copy-start.1
  0.7 0.0 copy-start
  0.7 0.0 copy-start.3
  0.7 1.9 %pack.1 = bf16[32,48,128]{2,1,0:T(8,128)(2,1)} custom-call(s32[8]{0:T(128)} %count_ref.7, bf16[1024,128]{1,0:T(8,128)(2,1)} %k_ref.3, bf16[1024,128]{1,0:T(8,128)(2,1)} %v_ref.3), custom_call_target="tpu_custom_call" | custom-call | tf_op jit(solution)/shard_map/pack/pallas_call | solution.py:51
  2.6 18.8 %all_to_all.20.in_ref.flag_ref = bf16[32,48,128]{2,1,0:T(8,128)(2,1)S(1)} all-to-all(bf16[32,48,128]{2,1,0:T(8,128)(2,1)} %pack.1), channel_id=1, replica_groups=mesh['ctx'=32,'head'=4,'rep'=1] {'ctx'}, dimensions={0} | all-to-all | bytes 786432 | tf_op jit(solution)/shard_map/all_to_all | solution.py:373
  21.4 0.1 stack.1
  21.5 13.8 %all_to_all.21.ext_ref = bf16[32,48,128]{2,1,0:T(8,128)(2,1)S(1)} all-to-all(bf16[32,48,128]{2,1,0:T(8,128)(2,1)S(1)} %stack.1), channel_id=1, replica_groups=mesh['ctx'=32,'head'=4,'rep'=1] {'ctx'}, dimensions={0} | all-to-all | bytes 786432 | tf_op jit(solution)/shard_map/all_to_all | solution.py:374
  35.2 0.0 copy-done.2
  35.2 0.0 copy-done.1
  35.2 0.0 copy-done
  35.2 0.0 copy-done.3
  35.2 15.0 %attention.1 = (bf16[8,896,1024]{2,1,0:T(8,128)(2,1)}, bf16[1792,128]{1,0:T(8,128)(2,1)S(1)}, f32[1024,128]{1,0:T(8,128)S(1)}, f32[1024,128]{1,0:T(8,128)S(1)}, bf16[32,48,128]{2,1,0:T(8,128)(2,1)}) custom-call(s32[8,6]{1,0:T(8,128)S(1)} %copy-done.3, s32[8]{0:T(128)S(1)} %copy-done.2, bf16[1024,1024]{1,0:T(8,128)(2,1)} %q_ref.1, bf16[1024,1024]{1,0:T(8,128)(2,1)} %o_ref.1, ...), custom_call_target="tpu_custom_call" | custom-call | tf_op jit(solution)/shard_map/attention/pallas_call | solution.py:283
  50.2 12.1 %all-to-all-start.2 = ((bf16[32,48,128]{2,1,0:T(8,128)(2,1)}), bf16[32,48,128]{2,1,0:T(8,128)(2,1)S(1)}, u32[]{:S(2)}, u32[]{:S(2)}) async-start(bf16[32,48,128]{2,1,0:T(8,128)(2,1)} %get-tuple-element.12), calls=%async_computation.2 | async-start | bytes 786432 | tf_op jit(solution)/shard_map/all_to_all | solution.py:378
  62.3 10.3 %query_grads.1 = bf16[1024,1024]{1,0:T(8,128)(2,1)} custom-call(s32[8,6]{1,0:T(8,128)S(1)} %copy-done.3, s32[8]{0:T(128)S(1)} %copy-done.2, bf16[8,896,1024]{2,1,0:T(8,128)(2,1)} %get-tuple-element.13.ds_ref, bf16[1792,128]{1,0:T(8,128)(2,1)S(1)} %get-tuple-element.14.kt_ref), custom_call_target="tpu_custom_call" | custom-call | flops 10000000000 | bytes 16777216 | tf_op jit(solution)/shard_map/query_grads/pallas_call | solution.py:350
  72.6 0.0 all-to-all-done.2.in_ref
  72.6 0.2 segsum.1
  72.7 17.7 %all_to_all.22.in_ref = bf16[32,48,128]{2,1,0:T(8,128)(2,1)S(1)} all-to-all(bf16[32,48,128]{2,1,0:T(8,128)(2,1)S(1)} %segsum.1), channel_id=1, replica_groups=mesh['ctx'=32,'head'=4,'rep'=1] {'ctx'}, dimensions={0} | all-to-all | bytes 786432 | tf_op jit(solution)/shard_map/all_to_all | solution.py:381
  90.4 1.5 %final.1 = (bf16[1024,128]{1,0:T(8,128)(2,1)}, bf16[1024,128]{1,0:T(8,128)(2,1)}) custom-call(s32[8]{0:T(128)S(1)} %copy-done.2, f32[1024,128]{1,0:T(8,128)S(1)} %get-tuple-element.16.dk_ref, f32[1024,128]{1,0:T(8,128)S(1)} %get-tuple-element.17.dv_ref, bf16[32,48,128]{2,1,0:T(8,128)(2,1)S(1)} %all_to_all.22.in_ref), custom_call_target="tpu_custom_call" | custom-call | tf_op jit(solution)/shard_map/final/pallas_call | solution.py:116
Async XLA Ops:
  0.6 34.6 %copy-start.2 = (s32[8]{0:T(128)S(1)}, s32[8]{0:T(128)}, u32[]{:S(2)}) copy-start(s32[8]{0:T(128)} %count_ref.7) | copy-start | bytes 100
  0.6 34.6 %copy-start.1 = (bf16[1024,128]{1,0:T(8,128)(2,1)S(1)}, bf16[1024,128]{1,0:T(8,128)(2,1)}, u32[]{:S(2)}) copy-start(bf16[1024,128]{1,0:T(8,128)(2,1)} %v_ref.3) | copy-start | bytes 786436
  0.7 34.6 %copy-start = (bf16[1024,128]{1,0:T(8,128)(2,1)S(1)}, bf16[1024,128]{1,0:T(8,128)(2,1)}, u32[]{:S(2)}) copy-start(bf16[1024,128]{1,0:T(8,128)(2,1)} %k_ref.3) | copy-start | bytes 786436
  0.7 34.6 %copy-start.3 = (s32[8,6]{1,0:T(8,128)S(1)}, s32[8,6]{1,0:T(8,128)}, u32[]{:S(2)}) copy-start(s32[8,6]{1,0:T(8,128)} %ids_ref.3) | copy-start | bytes 580
  50.2 22.4 %all-to-all-start.2 = ((bf16[32,48,128]{2,1,0:T(8,128)(2,1)}), bf16[32,48,128]{2,1,0:T(8,128)(2,1)S(1)}, u32[]{:S(2)}, u32[]{:S(2)}) async-start(bf16[32,48,128]{2,1,0:T(8,128)(2,1)} %get-tuple-element.12), calls=%async_computation.2 | async-start | bytes 786432 | tf_op jit(solution)/shard_map/all_to_all | solution.py:378

commit v6 on v4

--- a/solution.py
+++ b/solution.py
@@ -327,9 +327,25 @@
     )(ids, count, queries, grad_out, keys, values, ext)
 
 
-def query_kernel(ids_ref, count_ref, ds_ref, kt_ref, dq_ref, kb):
+def query_kernel(ids_ref, count_ref, ds_ref, kt_ref, dq_ref, kb, held, sems):
     b = pl.program_id(0)
     base = lax.axis_index("ctx") * OWN
+
+    def fetch(block, j):
+        rows = pl.ds(j * BLK, BLK)
+        return pltpu.make_async_copy(
+            ds_ref.at[block, rows, :], held.at[block, rows, :], sems.at[block, j]
+        )
+
+    @pl.when(b == 0)
+    def _():
+        for block in range(OWN):
+            for j in range(MAXA + 1):
+
+                @pl.when(j <= count_ref[block])
+                def _(block=block, j=j):
+                    fetch(block, j).start()
+
     count = count_ref[b]
     for n in range(MAXA + 1):
 
@@ -339,11 +355,13 @@
             places.append(pl.multiple_of(b * BLK, BLK))
             for j in range(n + 1):
                 kb[pl.ds(j * BLK, BLK), :] = kt_ref[pl.ds(places[j], BLK), :]
+            for j in range(n + 1):
+                fetch(b, j).wait()
             nk = (n + 1) * BLK
-            g = tn(kb[pl.ds(0, nk), :], ds_ref[0, pl.ds(0, nk), :]) * SCALE
+            g = (tn(kb[pl.ds(0, nk), :], held[b, pl.ds(0, nk), :]) * SCALE).astype(BF16)
             for h in range(HQ):
                 head = slice(h * HD, (h + 1) * HD)
-                dq_ref[:, head] = g[:, head].T.astype(BF16)
+                dq_ref[:, head] = g[:, head].T
 
 
 def query_grads(ids, count, dscores, table):
@@ -353,11 +371,15 @@
             num_scalar_prefetch=2,
             grid=(OWN,),
             in_specs=[
-                pl.BlockSpec((1, (MAXA + 1) * BLK, ROWS), lambda b, *_: (b, 0, 0)),
+                pl.BlockSpec(memory_space=pl.ANY),
                 pl.BlockSpec(table.shape, lambda b, *_: (0, 0)),
             ],
             out_specs=pl.BlockSpec((BLK, ROWS), lambda b, *_: (b, 0)),
-            scratch_shapes=[pltpu.VMEM(((MAXA + 1) * BLK, HD), BF16)],
+            scratch_shapes=[
+                pltpu.VMEM(((MAXA + 1) * BLK, HD), BF16),
+                pltpu.VMEM((OWN, (MAXA + 1) * BLK, ROWS), BF16),
+                pltpu.SemaphoreType.DMA((OWN, MAXA + 1)),
+            ],
         ),
         out_shape=jax.ShapeDtypeStruct((OWN * BLK, ROWS), BF16),
         compiler_params=pltpu.CompilerParams(vmem_limit_bytes=VMEM_Q),

time: 89 us -> 88.7 us (level); the launches traced: 88.1 us -> 89.1 us
  waiting for transfers between devices: 0.01 us -> 2.72 us
  Pallas kernels: 32 us -> 30.8 us
    pallas_call x1, Pallas kernels: 10.5 us -> 7.56 us  [query_grads(): pl.pallas_call(query_kernel, grid_spec=pltpu.PrefetchScalarGridSpec(num_s...]
    all_to_all x1, waiting for transfers between devices: 0.01 us -> 2.72 us  [body(): terms = lax.all_to_all(sums, 'ctx', 0, 0, tiled=True)]
    pallas_call x1, Pallas kernels: 17 us -> 18.8 us  [attention(): pl.pallas_call(attn_kernel, grid_spec=pltpu.PrefetchScalarGridSpec(num_sc...]
  transfers between devices with their start and end apart: 1 -> 1, of which waited for: 0 -> 1; matrix products, arithmetic and copies ran while one was open for 0% -> 0% of each run, Pallas kernels for 12% -> 8%
where the time goes in v6:
time: 88.7 us; the launch traced here: 89.1 us
  blocking collectives  50.8 us (57%)
  Pallas kernels  30.8 us (35%)
  starting transfers between devices  4.08 us (5%)
  waiting for transfers between devices  2.72 us (3%)
    pallas_call x1, Pallas kernels, attention(): pl.pallas_call(attn_kernel, grid_spec=pltpu.PrefetchScalarGridSpec(num_sc...  18.8 us
    all_to_all x1, blocking collectives, body(): pieces = lax.all_to_all(mine, 'ctx', 0, 0, tiled=True)  18.8 us
    all_to_all x1, blocking collectives, body(): sums = segsum(pieces, lax.all_to_all(back, 'ctx', 0, 0, tiled=True))  18.3 us
    all_to_all x1, blocking collectives, body(): ext = lax.all_to_all(stack(pieces), 'ctx', 0, 0, tiled=True)  13.8 us
    pallas_call x1, Pallas kernels, query_grads(): pl.pallas_call(query_kernel, grid_spec=pltpu.PrefetchScalarGridSpec(num_s...  7.56 us
    all_to_all x1, starting transfers between devices, body(): terms = lax.all_to_all(sums, 'ctx', 0, 0, tiled=True)  4.08 us
    all_to_all x1, waiting for transfers between devices, body(): terms = lax.all_to_all(sums, 'ctx', 0, 0, tiled=True)  2.72 us
    pallas_call x1, Pallas kernels, pack(): pl.pallas_call(pack_kernel, out_shape=jax.ShapeDtypeStruct((SHARDS, PIECE...  1.93 us
  transfers between devices with their start and end apart: 1, of which 1 were waited for; matrix products, arithmetic and copies ran while one was open for 0% of the time, Pallas kernels for 8%

profile of v6, /device:TPU:1, one launch (start us, length us, event | category | flops | bytes accessed | tf_op | source)
XLA Modules:
  0.0 89.1 jit_solution(6706013988102440897)
XLA Ops:
  0.6 0.0 copy-start.2
  0.6 0.0 copy-start
  0.7 0.0 copy-start.1
  0.7 0.0 copy-start.3
  0.7 1.9 %pack.1 = bf16[32,48,128]{2,1,0:T(8,128)(2,1)} custom-call(s32[8]{0:T(128)} %count_ref.7, bf16[1024,128]{1,0:T(8,128)(2,1)} %k_ref.3, bf16[1024,128]{1,0:T(8,128)(2,1)} %v_ref.3), custom_call_target="tpu_custom_call" | custom-call | tf_op jit(solution)/shard_map/pack/pallas_call | solution.py:51
  2.6 18.8 %all_to_all.20.in_ref.flag_ref = bf16[32,48,128]{2,1,0:T(8,128)(2,1)S(1)} all-to-all(bf16[32,48,128]{2,1,0:T(8,128)(2,1)} %pack.1), channel_id=1, replica_groups=mesh['ctx'=32,'head'=4,'rep'=1] {'ctx'}, dimensions={0} | all-to-all | bytes 786432 | tf_op jit(solution)/shard_map/all_to_all | solution.py:395
  21.4 0.1 stack.1
  21.5 13.8 %all_to_all.21.ext_ref = bf16[32,48,128]{2,1,0:T(8,128)(2,1)S(1)} all-to-all(bf16[32,48,128]{2,1,0:T(8,128)(2,1)S(1)} %stack.1), channel_id=1, replica_groups=mesh['ctx'=32,'head'=4,'rep'=1] {'ctx'}, dimensions={0} | all-to-all | bytes 786432 | tf_op jit(solution)/shard_map/all_to_all | solution.py:396
  35.2 0.0 copy-done.2
  35.2 0.0 copy-done
  35.2 0.0 copy-done.1
  35.2 0.0 copy-done.3
  35.2 18.8 %attention.1 = (bf16[8,896,1024]{2,1,0:T(8,128)(2,1)}, bf16[1792,128]{1,0:T(8,128)(2,1)S(1)}, f32[1024,128]{1,0:T(8,128)S(1)}, f32[1024,128]{1,0:T(8,128)S(1)}, bf16[32,48,128]{2,1,0:T(8,128)(2,1)S(1)}) custom-call(s32[8,6]{1,0:T(8,128)S(1)} %copy-done.3, s32[8]{0:T(128)S(1)} %copy-done.2, bf16[1024,1024]{1,0:T(8,128)(2,1)} %q_ref.1, ...), custom_call_target="tpu_custom_call" | custom-call | tf_op jit(solution)/shard_map/attention/pallas_call | solution.py:283
  54.1 18.3 %all_to_all.22.in_ref = bf16[32,48,128]{2,1,0:T(8,128)(2,1)S(1)} all-to-all(bf16[32,48,128]{2,1,0:T(8,128)(2,1)S(1)} %get-tuple-element.14), channel_id=1, replica_groups=mesh['ctx'=32,'head'=4,'rep'=1] {'ctx'}, dimensions={0} | all-to-all | bytes 786432 | tf_op jit(solution)/shard_map/all_to_all | solution.py:400
  72.3 0.9 %segsum.1 = bf16[32,48,128]{2,1,0:T(8,128)(2,1)} custom-call(bf16[32,48,128]{2,1,0:T(8,128)(2,1)S(1)} %all_to_all.20.in_ref.flag_ref, bf16[32,48,128]{2,1,0:T(8,128)(2,1)S(1)} %all_to_all.22.in_ref), custom_call_target="tpu_custom_call" | custom-call | tf_op jit(solution)/shard_map/segsum/pallas_call | solution.py:92
  73.3 4.1 %all-to-all-start.3 = ((bf16[32,48,128]{2,1,0:T(8,128)(2,1)}), bf16[32,48,128]{2,1,0:T(8,128)(2,1)S(1)}, u32[]{:S(2)}, u32[]{:S(2)}) async-start(bf16[32,48,128]{2,1,0:T(8,128)(2,1)} %segsum.1), calls=%async_computation.3 | async-start | bytes 786432 | tf_op jit(solution)/shard_map/all_to_all | solution.py:401
  77.3 7.6 %query_grads.1 = bf16[1024,1024]{1,0:T(8,128)(2,1)} custom-call(s32[8,6]{1,0:T(8,128)S(1)} %copy-done.3, s32[8]{0:T(128)S(1)} %copy-done.2, bf16[8,896,1024]{2,1,0:T(8,128)(2,1)} %get-tuple-element.10.ds_ref, bf16[1792,128]{1,0:T(8,128)(2,1)S(1)} %get-tuple-element.11.kt_ref), custom_call_target="tpu_custom_call" | custom-call | flops 10000000000 | bytes 16777216 | tf_op jit(solution)/shard_map/query_grads/pallas_call | solution.py:368
  84.9 2.7 %all-to-all-done.3.in_ref = bf16[32,48,128]{2,1,0:T(8,128)(2,1)S(1)} async-done(((bf16[32,48,128]{2,1,0:T(8,128)(2,1)}), bf16[32,48,128]{2,1,0:T(8,128)(2,1)S(1)}, u32[]{:S(2)}, u32[]{:S(2)}) %all-to-all-start.3) | async-done | bytes 393248 | tf_op jit(solution)/shard_map/all_to_all | solution.py:401
  87.6 1.5 %final.1 = (bf16[1024,128]{1,0:T(8,128)(2,1)}, bf16[1024,128]{1,0:T(8,128)(2,1)}) custom-call(s32[8]{0:T(128)S(1)} %copy-done.2, f32[1024,128]{1,0:T(8,128)S(1)} %get-tuple-element.12.dk_ref, f32[1024,128]{1,0:T(8,128)S(1)} %get-tuple-element.13.dv_ref, bf16[32,48,128]{2,1,0:T(8,128)(2,1)S(1)} %all-to-all-done.3.in_ref), custom_call_target="tpu_custom_call" | custom-call | tf_op jit(solution)/shard_map/final/pallas_call | solution.py:116
Async XLA Ops:
  0.6 34.6 %copy-start.2 = (s32[8]{0:T(128)S(1)}, s32[8]{0:T(128)}, u32[]{:S(2)}) copy-start(s32[8]{0:T(128)} %count_ref.7) | copy-start | bytes 100
  0.6 34.6 %copy-start = (bf16[1024,128]{1,0:T(8,128)(2,1)S(1)}, bf16[1024,128]{1,0:T(8,128)(2,1)}, u32[]{:S(2)}) copy-start(bf16[1024,128]{1,0:T(8,128)(2,1)} %k_ref.3) | copy-start | bytes 786436
  0.7 34.6 %copy-start.1 = (bf16[1024,128]{1,0:T(8,128)(2,1)S(1)}, bf16[1024,128]{1,0:T(8,128)(2,1)}, u32[]{:S(2)}) copy-start(bf16[1024,128]{1,0:T(8,128)(2,1)} %v_ref.3) | copy-start | bytes 786436
  0.7 34.6 %copy-start.3 = (s32[8,6]{1,0:T(8,128)S(1)}, s32[8,6]{1,0:T(8,128)}, u32[]{:S(2)}) copy-start(s32[8,6]{1,0:T(8,128)} %ids_ref.3) | copy-start | bytes 580
  73.3 14.4 %all-to-all-start.3 = ((bf16[32,48,128]{2,1,0:T(8,128)(2,1)}), bf16[32,48,128]{2,1,0:T(8,128)(2,1)S(1)}, u32[]{:S(2)}, u32[]{:S(2)}) async-start(bf16[32,48,128]{2,1,0:T(8,128)(2,1)} %segsum.1), calls=%async_computation.3 | async-start | bytes 786432 | tf_op jit(solution)/shard_map/all_to_all | solution.py:401

commit v7 on v6

--- a/solution.py
+++ b/solution.py
@@ -15,6 +15,7 @@
 SHARDS = 32
 ROWS = HQ * BLK
 CHUNK = 512
+PAIR = 2
 PIECE = 8 * MAXA
 MARK = 1e30
 MARK_MIN = 1e29
@@ -164,10 +165,10 @@
     dva,
     *slots,
 ):
-    b = pl.program_id(0)
+    step = pl.program_id(0)
     base = lax.axis_index("ctx") * OWN
 
-    @pl.when(b == 0)
+    @pl.when(step == 0)
     def _():
         kt[pl.ds(0, OWN * BLK), :] = k_ref[...]
         vt[pl.ds(0, OWN * BLK), :] = v_ref[...]
@@ -175,23 +176,28 @@
             piece = ext_ref[pl.ds(half * 16, 16)].astype(F32)
             for j in range(MAXA):
                 rows = piece[:, 8 * j : 8 * j + 8, :].reshape(BLK, HD)
+                rows = jnp.where(rows < MARK_MIN, rows, 0.0)
                 tab[pl.ds((OWN + j) * BLK, BLK), :] = rows.astype(BF16)
         dke[...] = jnp.zeros_like(dke)
         dve[...] = jnp.zeros_like(dve)
 
-    count = count_ref[b]
+    counts = [count_ref[step * PAIR + i] for i in range(PAIR)]
+    count = functools.reduce(jnp.maximum, counts)
+    per_block = ROWS // CHUNK
     coef = SCALE * LOG2E
     heads = CHUNK // HD
     key_pos = lax.broadcasted_iota(jnp.int32, (BLK, CHUNK), 0)
     row_pos = lax.rem(lax.broadcasted_iota(jnp.int32, (BLK, CHUNK), 1), BLK)
     causal = key_pos <= row_pos
 
-    def table_row(j):
-        return table_place(ids_ref, base, b, j)
+    def table_row(i, j):
+        return table_place(ids_ref, base, step * PAIR + i, j)
 
     def rows_of(ref, c):
+        block, c = divmod(c, per_block)
+        rows = pl.ds(block * BLK, BLK)
         return jnp.concatenate(
-            [ref[:, c * CHUNK + h * HD : c * CHUNK + (h + 1) * HD] for h in range(heads)], axis=0
+            [ref[rows, c * CHUNK + h * HD : c * CHUNK + (h + 1) * HD] for h in range(heads)], axis=0
         )
 
     def slot(c):
@@ -199,7 +205,9 @@
 
     def scores(n, c):
         nk = (n + 1) * BLK
-        return nt(kb[pl.ds(0, nk), :], rows_of(q_ref, c)), nt(vb[pl.ds(0, nk), :], rows_of(o_ref, c))
+        block = c // per_block
+        s = nt(kb[block, pl.ds(0, nk), :], rows_of(q_ref, c))
+        return s, nt(vb[block, pl.ds(0, nk), :], rows_of(o_ref, c))
 
     def keep(n, c, j, both):
         e_scr, d_scr, _ = slot(c)
@@ -210,6 +218,8 @@
         e = jnp.exp2((s - top) * coef)
         e_scr[pl.ds(j * BLK, BLK), :] = e
         d_scr[pl.ds(j * BLK, BLK), :] = d
+        if j < n:
+            top = jnp.where(j < counts[c // per_block], top, -MARK)
         return top, jnp.sum(e, axis=0, keepdims=True), jnp.sum(e * d, axis=0, keepdims=True)
 
     def merge(c, stats):
@@ -222,34 +232,42 @@
             g_scr[j : j + 1, :] = f * inv
         g_scr[MAXA + 1 : MAXA + 2, :] = delta
 
-    def weigh(c, j):
+    def weigh(n, c, j):
         e_scr, d_scr, g_scr = slot(c)
         p = e_scr[pl.ds(j * BLK, BLK), :] * g_scr[j : j + 1, :]
         ds = p * (d_scr[pl.ds(j * BLK, BLK), :] - g_scr[MAXA + 1 : MAXA + 2, :])
         ds = ds.astype(BF16)
-        ds_ref[0, pl.ds(j * BLK, BLK), c * CHUNK : (c + 1) * CHUNK] = ds
+        block, c = divmod(c, per_block)
+        row = pl.multiple_of(counts[block] * BLK, BLK) if j == n else j * BLK
+        ds_ref[block, pl.ds(row, BLK), c * CHUNK : (c + 1) * CHUNK] = ds
         return p.astype(BF16), ds
 
     def add(n, c, tiles):
         nk = (n + 1) * BLK
         dv = nn(jnp.concatenate([p for p, _ in tiles], axis=0), rows_of(o_ref, c))
         dk = nn(jnp.concatenate([ds for _, ds in tiles], axis=0), rows_of(q_ref, c))
+        block, c = divmod(c, per_block)
         if c == 0:
-            dva[pl.ds(0, nk), :] = dv
-            dka[pl.ds(0, nk), :] = dk
+            dva[block, pl.ds(0, nk), :] = dv
+            dka[block, pl.ds(0, nk), :] = dk
         else:
-            dva[pl.ds(0, nk), :] += dv
-            dka[pl.ds(0, nk), :] += dk
+            dva[block, pl.ds(0, nk), :] += dv
+            dka[block, pl.ds(0, nk), :] += dk
 
     for n in range(MAXA + 1):
 
         @pl.when(count == n)
         def _(n=n):
-            places = [table_row(j) for j in range(n)] + [pl.multiple_of(b * BLK, BLK)]
-            for j in range(n + 1):
-                kb[pl.ds(j * BLK, BLK), :] = kt[pl.ds(places[j], BLK), :]
-                vb[pl.ds(j * BLK, BLK), :] = vt[pl.ds(places[j], BLK), :]
-            chunks = ROWS // CHUNK
+            places = [
+                [table_row(i, j) for j in range(n)]
+                + [pl.multiple_of((step * PAIR + i) * BLK, BLK)]
+                for i in range(PAIR)
+            ]
+            for i in range(PAIR):
+                for j in range(n + 1):
+                    kb[i, pl.ds(j * BLK, BLK), :] = kt[pl.ds(places[i][j], BLK), :]
+                    vb[i, pl.ds(j * BLK, BLK), :] = vt[pl.ds(places[i][j], BLK), :]
+            chunks = PAIR * per_block
             both = scores(n, 0)
             merge(0, [keep(n, 0, j, both) for j in range(n + 1)])
             for c in range(chunks):
@@ -258,17 +276,18 @@
                     both = scores(n, c + 1)
                 tiles, stats = [], []
                 for j in range(n + 1):
-                    tiles.append(weigh(c, j))
+                    tiles.append(weigh(n, c, j))
                     if more:
                         stats.append(keep(n, c + 1, j, both))
                 add(n, c, tiles)
                 if more:
                     merge(c + 1, stats)
-            for j in range(n + 1):
-                dke[pl.ds(places[j], BLK), :] += dka[pl.ds(j * BLK, BLK), :]
-                dve[pl.ds(places[j], BLK), :] += dva[pl.ds(j * BLK, BLK), :]
-
-    @pl.when(b == OWN - 1)
+            for i in range(PAIR):
+                for j in range(n + 1):
+                    dke[pl.ds(places[i][j], BLK), :] += dka[i, pl.ds(j * BLK, BLK), :]
+                    dve[pl.ds(places[i][j], BLK), :] += dva[i, pl.ds(j * BLK, BLK), :]
+
+    @pl.when(step == OWN // PAIR - 1)
     def _():
         dk_ref[...] = dke[pl.ds(0, OWN * BLK), :]
         dv_ref[...] = dve[pl.ds(0, OWN * BLK), :]
@@ -284,16 +303,16 @@
         attn_kernel,
         grid_spec=pltpu.PrefetchScalarGridSpec(
             num_scalar_prefetch=2,
-            grid=(OWN,),
+            grid=(OWN // PAIR,),
             in_specs=[
-                pl.BlockSpec((BLK, ROWS), lambda b, *_: (b, 0)),
-                pl.BlockSpec((BLK, ROWS), lambda b, *_: (b, 0)),
+                pl.BlockSpec((PAIR * BLK, ROWS), lambda b, *_: (b, 0)),
+                pl.BlockSpec((PAIR * BLK, ROWS), lambda b, *_: (b, 0)),
                 whole((OWN * BLK, HD)),
                 whole((OWN * BLK, HD)),
                 whole((SHARDS, PIECE, HD)),
             ],
             out_specs=[
-                pl.BlockSpec((1, (MAXA + 1) * BLK, ROWS), lambda b, *_: (b, 0, 0)),
+                pl.BlockSpec((PAIR, (MAXA + 1) * BLK, ROWS), lambda b, *_: (b, 0, 0)),
                 whole((tiles * BLK, HD)),
                 whole((OWN * BLK, HD)),
                 whole((OWN * BLK, HD)),
@@ -303,10 +322,10 @@
                 pltpu.VMEM((tiles * BLK, HD), BF16),
                 pltpu.VMEM((tiles * BLK, HD), F32),
                 pltpu.VMEM((tiles * BLK, HD), F32),
-                pltpu.VMEM(((MAXA + 1) * BLK, HD), BF16),
-                pltpu.VMEM(((MAXA + 1) * BLK, HD), BF16),
-                pltpu.VMEM(((MAXA + 1) * BLK, HD), F32),
-                pltpu.VMEM(((MAXA + 1) * BLK, HD), F32),
+                pltpu.VMEM((PAIR, (MAXA + 1) * BLK, HD), BF16),
+                pltpu.VMEM((PAIR, (MAXA + 1) * BLK, HD), BF16),
+                pltpu.VMEM((PAIR, (MAXA + 1) * BLK, HD), F32),
+                pltpu.VMEM((PAIR, (MAXA + 1) * BLK, HD), F32),
             ]
             + [
                 pltpu.VMEM(((MAXA + 1) * BLK, CHUNK), F32),

time: 88.7 us -> 93.3 us (1.052)
  blocking collectives: 50.8 us -> 56.3 us
  Pallas kernels: 30.8 us -> 29.3 us
    all_to_all x1, blocking collectives: 18.3 us -> 23.8 us  [body(): sums = segsum(pieces, lax.all_to_all(back, 'ctx', 0, 0, tiled=True))]
    pallas_call x1, Pallas kernels: 18.8 us -> 17.6 us  [attention(): pl.pallas_call(attn_kernel, grid_spec=pltpu.PrefetchScalarGridSpec(num_sc...]
where the time goes in v7:
time: 93.3 us
  blocking collectives  56.3 us (60%)
  Pallas kernels  29.3 us (31%)
  starting transfers between devices  3.9 us (4%)
  waiting for transfers between devices  3.01 us (3%)
    all_to_all x1, blocking collectives, body(): sums = segsum(pieces, lax.all_to_all(back, 'ctx', 0, 0, tiled=True))  23.8 us
    all_to_all x1, blocking collectives, body(): pieces = lax.all_to_all(mine, 'ctx', 0, 0, tiled=True)  18.8 us
    pallas_call x1, Pallas kernels, attention(): pl.pallas_call(attn_kernel, grid_spec=pltpu.PrefetchScalarGridSpec(num_sc...  17.6 us
    all_to_all x1, blocking collectives, body(): ext = lax.all_to_all(stack(pieces), 'ctx', 0, 0, tiled=True)  13.8 us
    pallas_call x1, Pallas kernels, query_grads(): pl.pallas_call(query_kernel, grid_spec=pltpu.PrefetchScalarGridSpec(num_s...  7.26 us
    all_to_all x1, starting transfers between devices, body(): terms = lax.all_to_all(sums, 'ctx', 0, 0, tiled=True)  3.9 us
    all_to_all x1, waiting for transfers between devices, body(): terms = lax.all_to_all(sums, 'ctx', 0, 0, tiled=True)  3.01 us
    pallas_call x1, Pallas kernels, pack(): pl.pallas_call(pack_kernel, out_shape=jax.ShapeDtypeStruct((SHARDS, PIECE...  1.93 us
  transfers between devices with their start and end apart: 1, of which 1 were waited for; matrix products, arithmetic and copies ran while one was open for 0% of the time, Pallas kernels for 8%

profile of v7, /device:TPU:1, one launch (start us, length us, event | category | flops | bytes accessed | tf_op | source)
XLA Modules:
  0.0 93.3 jit_solution(11688840971579634131)
XLA Ops:
  0.6 0.0 copy-start.2
  0.6 0.0 copy-start
  0.7 0.0 copy-start.1
  0.7 0.0 copy-start.3
  0.7 1.9 %pack.1 = bf16[32,48,128]{2,1,0:T(8,128)(2,1)} custom-call(s32[8]{0:T(128)} %count_ref.7, bf16[1024,128]{1,0:T(8,128)(2,1)} %k_ref.3, bf16[1024,128]{1,0:T(8,128)(2,1)} %v_ref.3), custom_call_target="tpu_custom_call" | custom-call | tf_op jit(solution)/shard_map/pack/pallas_call | solution.py:52
  2.6 18.8 %all_to_all.20.in_ref.flag_ref = bf16[32,48,128]{2,1,0:T(8,128)(2,1)S(1)} all-to-all(bf16[32,48,128]{2,1,0:T(8,128)(2,1)} %pack.1), channel_id=1, replica_groups=mesh['ctx'=32,'head'=4,'rep'=1] {'ctx'}, dimensions={0} | all-to-all | bytes 786432 | tf_op jit(solution)/shard_map/all_to_all | solution.py:414
  21.4 0.1 stack.1
  21.5 13.8 %all_to_all.21.ext_ref = bf16[32,48,128]{2,1,0:T(8,128)(2,1)S(1)} all-to-all(bf16[32,48,128]{2,1,0:T(8,128)(2,1)S(1)} %stack.1), channel_id=1, replica_groups=mesh['ctx'=32,'head'=4,'rep'=1] {'ctx'}, dimensions={0} | all-to-all | bytes 786432 | tf_op jit(solution)/shard_map/all_to_all | solution.py:415
  35.2 0.0 copy-done.2
  35.2 0.0 copy-done
  35.2 0.0 copy-done.1
  35.2 0.0 copy-done.3
  35.2 17.6 %attention.1 = (bf16[8,896,1024]{2,1,0:T(8,128)(2,1)}, bf16[1792,128]{1,0:T(8,128)(2,1)S(1)}, f32[1024,128]{1,0:T(8,128)S(1)}, f32[1024,128]{1,0:T(8,128)S(1)}, bf16[32,48,128]{2,1,0:T(8,128)(2,1)S(1)}) custom-call(s32[8,6]{1,0:T(8,128)S(1)} %copy-done.3, s32[8]{0:T(128)S(1)} %copy-done.2, bf16[1024,1024]{1,0:T(8,128)(2,1)} %q_ref.1, ...), custom_call_target="tpu_custom_call" | custom-call | tf_op jit(solution)/shard_map/attention/pallas_call | solution.py:302
  52.8 23.8 %all_to_all.22.in_ref = bf16[32,48,128]{2,1,0:T(8,128)(2,1)S(1)} all-to-all(bf16[32,48,128]{2,1,0:T(8,128)(2,1)S(1)} %get-tuple-element.14), channel_id=1, replica_groups=mesh['ctx'=32,'head'=4,'rep'=1] {'ctx'}, dimensions={0} | all-to-all | bytes 786432 | tf_op jit(solution)/shard_map/all_to_all | solution.py:419
  76.6 0.9 segsum.1
  77.6 3.9 %all-to-all-start.3 = ((bf16[32,48,128]{2,1,0:T(8,128)(2,1)}), bf16[32,48,128]{2,1,0:T(8,128)(2,1)S(1)}, u32[]{:S(2)}, u32[]{:S(2)}) async-start(bf16[32,48,128]{2,1,0:T(8,128)(2,1)} %segsum.1), calls=%async_computation.3 | async-start | bytes 786432 | tf_op jit(solution)/shard_map/all_to_all | solution.py:420
  81.5 7.3 %query_grads.1 = bf16[1024,1024]{1,0:T(8,128)(2,1)} custom-call(s32[8,6]{1,0:T(8,128)S(1)} %copy-done.3, s32[8]{0:T(128)S(1)} %copy-done.2, bf16[8,896,1024]{2,1,0:T(8,128)(2,1)} %get-tuple-element.10.ds_ref, bf16[1792,128]{1,0:T(8,128)(2,1)S(1)} %get-tuple-element.11.kt_ref), custom_call_target="tpu_custom_call" | custom-call | flops 10000000000 | bytes 16777216 | tf_op jit(solution)/shard_map/query_grads/pallas_call | solution.py:387
  88.7 3.0 %all-to-all-done.3.in_ref = bf16[32,48,128]{2,1,0:T(8,128)(2,1)S(1)} async-done(((bf16[32,48,128]{2,1,0:T(8,128)(2,1)}), bf16[32,48,128]{2,1,0:T(8,128)(2,1)S(1)}, u32[]{:S(2)}, u32[]{:S(2)}) %all-to-all-start.3) | async-done | bytes 393248 | tf_op jit(solution)/shard_map/all_to_all | solution.py:420
  91.8 1.5 %final.1 = (bf16[1024,128]{1,0:T(8,128)(2,1)}, bf16[1024,128]{1,0:T(8,128)(2,1)}) custom-call(s32[8]{0:T(128)S(1)} %copy-done.2, f32[1024,128]{1,0:T(8,128)S(1)} %get-tuple-element.12.dk_ref, f32[1024,128]{1,0:T(8,128)S(1)} %get-tuple-element.13.dv_ref, bf16[32,48,128]{2,1,0:T(8,128)(2,1)S(1)} %all-to-all-done.3.in_ref), custom_call_target="tpu_custom_call" | custom-call | tf_op jit(solution)/shard_map/final/pallas_call | solution.py:117
Async XLA Ops:
  0.6 34.6 %copy-start.2 = (s32[8]{0:T(128)S(1)}, s32[8]{0:T(128)}, u32[]{:S(2)}) copy-start(s32[8]{0:T(128)} %count_ref.7) | copy-start | bytes 100
  0.6 34.6 %copy-start = (bf16[1024,128]{1,0:T(8,128)(2,1)S(1)}, bf16[1024,128]{1,0:T(8,128)(2,1)}, u32[]{:S(2)}) copy-start(bf16[1024,128]{1,0:T(8,128)(2,1)} %k_ref.3) | copy-start | bytes 786436
  0.7 34.6 %copy-start.1 = (bf16[1024,128]{1,0:T(8,128)(2,1)S(1)}, bf16[1024,128]{1,0:T(8,128)(2,1)}, u32[]{:S(2)}) copy-start(bf16[1024,128]{1,0:T(8,128)(2,1)} %v_ref.3) | copy-start | bytes 786436
  0.7 34.6 %copy-start.3 = (s32[8,6]{1,0:T(8,128)S(1)}, s32[8,6]{1,0:T(8,128)}, u32[]{:S(2)}) copy-start(s32[8,6]{1,0:T(8,128)} %ids_ref.3) | copy-start | bytes 580
  77.6 14.2 %all-to-all-start.3 = ((bf16[32,48,128]{2,1,0:T(8,128)(2,1)}), bf16[32,48,128]{2,1,0:T(8,128)(2,1)S(1)}, u32[]{:S(2)}, u32[]{:S(2)}) async-start(bf16[32,48,128]{2,1,0:T(8,128)(2,1)} %segsum.1), calls=%async_computation.3 | async-start | bytes 786432 | tf_op jit(solution)/shard_map/all_to_all | solution.py:420
